TPU v7x, 128 devices: a whole 4x4x4 slice. The times are simulated.
128 devices in a mesh: expert: 16 (over z, y), dp: 8 (over x, core).
Axes of the slice: x: 4, y: 4, z: 4, core: 2. Of those that a mesh axis runs over, the one named last changes fastest.
Arguments:
- tokens: bfloat16 [32768, 2048], P(('expert', 'dp')), may hold values from -6 to 6
- grad_out: bfloat16 [32768, 2048], P(('expert', 'dp')), may hold values from -3 to 3
- scores: float32 [32, 128], P('expert'), may hold values from 0.2 to 1
- chosen: int32 [32, 128], replicated, may hold values from 0 to 32767, as said below
- gate_vals: bfloat16 [32, 64, 2, 128, 128], P('expert', 'dp'), may hold values from -0.375 to 0.375
- up_vals: bfloat16 [32, 64, 2, 128, 128], P('expert', 'dp'), may hold values from -0.375 to 0.375
- down_vals: bfloat16 [32, 64, 2, 128, 128], P('expert', 'dp'), may hold values from -0.375 to 0.375
- gate_rows: int32 [32, 64, 2], P('expert', 'dp'), may hold values from 0 to 15, all different within a row
- down_cols: int32 [32, 64, 2], P('expert', 'dp'), may hold values from 0 to 15, all different within a row
Outputs:
- grad_tokens: bfloat16 [32768, 2048], P(('expert', 'dp'))
- grad_gate: float32 [32, 64, 2, 128, 128], P('expert', 'dp')
- grad_up: float32 [32, 64, 2, 128, 128], P('expert', 'dp')
- grad_down: float32 [32, 64, 2, 128, 128], P('expert', 'dp')
- grad_scores: float32 [32, 128], P('expert')
Inputs may be any that keep to these rules, and one draw needn't show every extreme that they name: `chosen`: each row is ascending without repeats. Expert e takes between 0 and 2 tokens from the 256 tokens of one device (rows d * 256 to (d + 1) * 256 - 1), and exactly 2 from at least one device.
All inputs are finite; a program needn't handle non-finite values.
Results may differ from a plain program's by a relative error of at most 0.0057.
Values may be sent and summed in bfloat16 or wider, within the bound.
A program may use at most 128 MiB of HBM per device.

v0:
```python
import jax
import jax.numpy as jnp
from jax import lax
from jax.sharding import PartitionSpec as P


def expert_part(
    rows_in, rows_grad, row_scores, gate_block, up_block, down_block, in_blocks, out_blocks
):
    row_count, feat_width = rows_in.shape
    hid_blocks, link_count, block_size, _ = gate_block.shape
    block_count = feat_width // block_size
    picked_in = jnp.take(
        rows_in.reshape(row_count, block_count, block_size), in_blocks.reshape(-1), axis=1
    )
    picked_in = picked_in.reshape(row_count, hid_blocks, link_count, block_size)
    picked_out = jnp.take(
        rows_grad.reshape(row_count, block_count, block_size), out_blocks.reshape(-1), axis=1
    )
    picked_out = picked_out.reshape(row_count, hid_blocks, link_count, block_size)
    gate_pre = jnp.einsum(
        "rhkc,hkcf->rhf", picked_in, gate_block, preferred_element_type=jnp.float32
    )
    up_pre = jnp.einsum("rhkc,hkcf->rhf", picked_in, up_block, preferred_element_type=jnp.float32)
    gate_sig = jax.nn.sigmoid(gate_pre)
    gate_act = gate_pre * gate_sig
    hidden = (gate_act * up_pre).astype(jnp.bfloat16)
    out_terms = jnp.einsum("rhf,hkfc->rhkc", hidden, down_block, preferred_element_type=jnp.float32)
    score_grad = jnp.sum(picked_out.astype(jnp.float32) * out_terms, axis=(1, 2, 3))
    scaled = (row_scores[:, None, None, None] * picked_out).astype(jnp.bfloat16)
    hidden_back = jnp.einsum(
        "rhkc,hkfc->rhf", scaled, down_block, preferred_element_type=jnp.float32
    )
    down_grad = jnp.einsum("rhf,rhkc->hkfc", hidden, scaled, preferred_element_type=jnp.float32)
    up_back = (hidden_back * gate_act).astype(jnp.bfloat16)
    gate_back = (hidden_back * up_pre * gate_sig * (1.0 + gate_pre * (1.0 - gate_sig))).astype(
        jnp.bfloat16
    )
    gate_grad = jnp.einsum(
        "rhkc,rhf->hkcf", picked_in, gate_back, preferred_element_type=jnp.float32
    )
    up_grad = jnp.einsum("rhkc,rhf->hkcf", picked_in, up_back, preferred_element_type=jnp.float32)
    in_terms = jnp.einsum(
        "rhf,hkcf->rhkc", gate_back, gate_block, preferred_element_type=jnp.float32
    )
    in_terms = in_terms + jnp.einsum(
        "rhf,hkcf->rhkc", up_back, up_block, preferred_element_type=jnp.float32
    )
    input_grad = jnp.zeros((row_count, block_count, block_size), jnp.float32)
    input_grad = input_grad.at[:, in_blocks.reshape(-1)].add(
        in_terms.reshape(row_count, hid_blocks * link_count, block_size)
    )
    return (input_grad.reshape(row_count, feat_width), gate_grad, up_grad, down_grad, score_grad)


def on_device(
    tokens, grad_out, scores, chosen, gate_vals, up_vals, down_vals, gate_rows, down_cols
):
    n_groups = lax.axis_size("expert")
    n_members = lax.axis_size("dp")
    n_devices = n_groups * n_members
    tok_count, feat_width = tokens.shape
    all_experts, capacity = chosen.shape
    per_group = scores.shape[0]
    slots = 2 * capacity // n_devices
    my_index = lax.axis_index("expert") * n_members + lax.axis_index("dp")
    lane_ids = jnp.arange(slots, dtype=jnp.int32)
    owners = chosen // tok_count
    counts = jnp.sum((owners == my_index).astype(jnp.int32), axis=1)
    before = jnp.sum((owners < my_index).astype(jnp.int32), axis=1)
    places = jnp.clip(before[:, None] + lane_ids[None, :], 0, capacity - 1)
    filled = lane_ids[None, :] < counts[:, None]
    local_ids = jnp.where(
        filled, jnp.take_along_axis(chosen, places, axis=1) - my_index * tok_count, 0
    )
    zero_value = jnp.zeros((), jnp.bfloat16)
    sent_in = jnp.where(filled[:, :, None], tokens[local_ids], zero_value).reshape(
        n_groups, per_group, slots, feat_width
    )
    sent_grad = jnp.where(filled[:, :, None], grad_out[local_ids], zero_value).reshape(
        n_groups, per_group, slots, feat_width
    )

    def copies(source_array):
        shaped = jnp.broadcast_to(
            source_array[:, None], (n_groups, n_members) + source_array.shape[1:]
        )
        return shaped.reshape((n_devices,) + source_array.shape[1:])

    recv_in, recv_grad = (
        lax.all_to_all(copies(sent_in), ("expert", "dp"), split_axis=0, concat_axis=2, tiled=True),
        lax.all_to_all(
            copies(sent_grad), ("expert", "dp"), split_axis=0, concat_axis=2, tiled=True
        ),
    )
    source_grid = (
        jnp.arange(n_groups, dtype=jnp.int32)[:, None] * n_members
        + jnp.arange(n_members, dtype=jnp.int32)[None, :]
    )
    recv_in = recv_in.reshape(per_group, n_devices * slots, feat_width)
    recv_grad = recv_grad.reshape(per_group, n_devices * slots, feat_width)
    sources = source_grid.reshape(-1)
    block_of = jnp.argsort(sources)
    first_expert = lax.axis_index("expert") * per_group
    mine_ids = lax.dynamic_slice_in_dim(chosen, first_expert, per_group, 0)
    mine_owner = mine_ids // tok_count
    per_source = jnp.sum(
        (mine_owner[:, :, None] == jnp.arange(n_devices, dtype=jnp.int32)[None, None, :]).astype(
            jnp.int32
        ),
        axis=1,
    )
    offsets = jnp.cumsum(per_source, axis=1) - per_source
    block_count = per_source[:, sources]
    block_start = offsets[:, sources]
    slot_places = jnp.clip(
        block_start[:, :, None] + lane_ids[None, None, :], 0, capacity - 1
    ).reshape(per_group, -1)
    slot_live = (lane_ids[None, None, :] < block_count[:, :, None]).reshape(per_group, -1)
    slot_scores = jnp.where(slot_live, jnp.take_along_axis(scores, slot_places, axis=1), 0.0)
    results = []
    for member in range(per_group):
        results.append(
            expert_part(
                recv_in[member],
                recv_grad[member],
                slot_scores[member],
                gate_vals[member],
                up_vals[member],
                down_vals[member],
                gate_rows[member],
                down_cols[member],
            )
        )
    partial_grad = jnp.stack([outcome[0] for outcome in results])
    grad_gate = jnp.stack([outcome[1] for outcome in results])
    grad_up = jnp.stack([outcome[2] for outcome in results])
    grad_down = jnp.stack([outcome[3] for outcome in results])
    score_parts = jnp.stack([outcome[4] for outcome in results])
    score_whole = lax.psum(score_parts, "dp")
    slot_rows = block_of[mine_owner] * slots + (
        jnp.arange(capacity, dtype=jnp.int32)[None, :]
        - jnp.take_along_axis(offsets, mine_owner, axis=1)
    )
    grad_scores = jnp.take_along_axis(score_whole, slot_rows, axis=1)
    returned = lax.all_to_all(
        partial_grad, ("expert", "dp"), split_axis=1, concat_axis=0, tiled=True
    )
    summed = jnp.sum(returned.reshape(n_groups, n_members, per_group * slots, feat_width), axis=1)
    values = jnp.where(filled[:, :, None], summed.reshape(all_experts, slots, feat_width), 0.0)
    grad_tokens = (
        jnp.zeros((tok_count, feat_width), jnp.float32)
        .at[local_ids.reshape(-1)]
        .add(values.reshape(-1, feat_width))
    )
    return (grad_tokens.astype(jnp.bfloat16), grad_gate, grad_up, grad_down, grad_scores)


def solution(mesh):
    placed = (
        P(("expert", "dp"), None),
        P(("expert", "dp"), None),
        P("expert", None),
        P(),
        P("expert", "dp", None, None, None),
        P("expert", "dp", None, None, None),
        P("expert", "dp", None, None, None),
        P("expert", "dp", None),
        P("expert", "dp", None),
    )
    return jax.shard_map(
        on_device,
        mesh=mesh,
        in_specs=placed,
        out_specs=(
            P(("expert", "dp"), None),
            P("expert", "dp", None, None, None),
            P("expert", "dp", None, None, None),
            P("expert", "dp", None, None, None),
            P("expert", None),
        ),
        check_vma=False,
    )
```

profile of v0, /device:TPU:0, one launch (start us, length us, event | category | flops | bytes accessed | tf_op | source)
XLA Modules:
  0.0 245.4 jit_solution(8619198542762993377)
XLA Ops:
  5.5 3.4 %broadcast_in_dim.109 = bf16[16,8,2,2,2048]{4,3,2,1,0:T(2,128)(2,1)} broadcast(bf16[16,2,2,2048]{3,2,1,0:T(2,128)(2,1)S(1)} %get-tuple-element.57), dimensions={0,2,3,4} | broadcast | bytes 2359296 | tf_op jit(solution)/shard_map/broadcast_in_dim | solution.py:85
  9.0 11.1 %all-to-all-start.1 = ((bf16[128,2,2,2048]{3,2,1,0:T(2,128)(2,1)}), bf16[128,2,2,2048]{3,2,1,0:T(2,128)(2,1)S(1)}, u32[]{:S(2)}, u32[]{:S(2)}) async-start(bf16[128,2,2,2048]{3,2,1,0:T(2,128)(2,1)} %bitcast.263), calls=%async_computation.1 | async-start | bytes 4194304 | tf_op jit(solution)/shard_map/all_to_all | solution.py:91
  23.9 4.7 %gather_fusion.6 = f32[512]{0:T(512)S(1)} fusion(f32[2,128]{1,0:T(2,128)S(1)} %copy-done.3, s32[512]{0:T(512)S(1)} %bitcast.243), kind=kCustom, calls=%fused_computation.10 | custom fusion | bytes 8192 | tf_op jit(solution)/shard_map/jit(take_along_axis)/gather | solution.py:120
  29.0 21.5 %all-to-all-done.1 = bf16[128,2,2,2048]{3,2,1,0:T(2,128)(2,1)S(1)} async-done(((bf16[128,2,2,2048]{3,2,1,0:T(2,128)(2,1)}), bf16[128,2,2,2048]{3,2,1,0:T(2,128)(2,1)S(1)}, u32[]{:S(2)}, u32[]{:S(2)}) %all-to-all-start.1) | async-done | bytes 2097184 | tf_op jit(solution)/shard_map/all_to_all | solution.py:91
  50.5 3.4 %broadcast_in_dim.108 = bf16[16,8,2,2,2048]{4,3,2,1,0:T(2,128)(2,1)} broadcast(bf16[16,2,2,2048]{3,2,1,0:T(2,128)(2,1)S(1)} %get-tuple-element.56), dimensions={0,2,3,4} | broadcast | bytes 2359296 | tf_op jit(solution)/shard_map/broadcast_in_dim | solution.py:85
  53.9 6.0 %all-to-all-start = ((bf16[128,2,2,2048]{3,2,1,0:T(2,128)(2,1)}), bf16[128,2,2,2048]{3,2,1,0:T(2,128)(2,1)}, u32[]{:S(2)}, u32[]{:S(2)}) async-start(bf16[128,2,2,2048]{3,2,1,0:T(2,128)(2,1)} %bitcast.264), calls=%async_computation | async-start | bytes 4194304 | tf_op jit(solution)/shard_map/all_to_all | solution.py:92
  59.9 2.9 %fusion.52 = (bf16[1,1,128,2,2048]{4,3,1,2,0:T(2,128)(2,1)}, bf16[1,1,128,2,2048]{4,3,1,2,0:T(2,128)(2,1)}) fusion(bf16[1,2,128,2,2048]{4,3,1,2,0:T(2,128)(2,1)S(1)} %bitcast.262), kind=kLoop, calls=%fused_computation.160 | loop fusion | bytes 4194304 | tf_op jit(solution)/shard_map/slice | solution.py:125
  68.6 2.9 %gather_fusion.12 = bf16[16,256,128]{2,1,0:T(8,128)(2,1)} fusion(bf16[256,16,128]{2,0,1:T(8,128)(2,1)} %copy.165, s32[1024]{0:T(1024)S(1)} %pad_clamp_fusion.1), kind=kCustom, calls=%fused_computation.3.clone | custom fusion | bytes 2097216 | tf_op jit(solution)/shard_map/jit(_take)/gather | solution.py:13
  78.5 11.2 %all-to-all-done = bf16[128,2,2,2048]{3,2,1,0:T(2,128)(2,1)} async-done(((bf16[128,2,2,2048]{3,2,1,0:T(2,128)(2,1)}), bf16[128,2,2,2048]{3,2,1,0:T(2,128)(2,1)}, u32[]{:S(2)}, u32[]{:S(2)}) %all-to-all-start) | async-done | bytes 2097184 | tf_op jit(solution)/shard_map/all_to_all | solution.py:92
  89.7 3.6 %fusion.51 = (bf16[1,1,128,2,2048]{4,3,1,2,0:T(2,128)(2,1)}, bf16[1,1,128,2,2048]{4,3,1,2,0:T(2,128)(2,1)}) fusion(bf16[1,2,128,2,2048]{4,3,1,2,0:T(2,128)(2,1)} %bitcast.9), kind=kLoop, calls=%fused_computation.159 | loop fusion | bytes 4194304 | tf_op jit(solution)/shard_map/slice | solution.py:126
  93.3 2.5 %reshape_squeeze.31 = bf16[256,16,128]{2,1,0:T(8,128)(2,1)} reshape(bf16[1,1,128,2,2048]{4,3,1,2,0:T(2,128)(2,1)} %get-tuple-element.50) | data formatting | bytes 2097152 | tf_op jit(solution)/shard_map/reshape;squeeze | solution.py:18
  98.3 2.9 %gather_fusion.9 = bf16[16,256,128]{2,1,0:T(8,128)(2,1)} fusion(bf16[256,16,128]{2,0,1:T(8,128)(2,1)} %copy.153, s32[1024]{0:T(1024)S(1)} %pad_clamp_fusion.4), kind=kCustom, calls=%fused_computation.clone | custom fusion | bytes 2097216 | tf_op jit(solution)/shard_map/jit(_take)/gather | solution.py:17
  101.1 2.8 %bitcast_convert_fusion.1 = f32[256,16,128]{2,0,1:T(8,128)} fusion(bf16[16,256,128]{2,1,0:T(8,128)(2,1)} %gather_fusion.9, pred[16]{0:T(512)(128)(4,1)S(1)} %compare_and_fusion.3), kind=kLoop, calls=%fused_computation.39 | loop fusion | flops 1048576 | bytes 3145744 | tf_op jit(solution)/shard_map/convert_element_type | solution.py:30
  103.9 2.9 %copy.154 = f32[256,16,128]{0,2,1:T(8,128)} copy(f32[256,16,128]{2,0,1:T(8,128)} %bitcast_convert_fusion.1) | data formatting | bytes 4194304 | tf_op jit(solution)/shard_map/convert_element_type | solution.py:30
  106.8 2.5 %reshape_squeeze.36 = bf16[256,16,128]{2,1,0:T(8,128)(2,1)} reshape(bf16[1,1,128,2,2048]{4,3,1,2,0:T(2,128)(2,1)} %get-tuple-element.51) | data formatting | bytes 2097152 | tf_op jit(solution)/shard_map/reshape;squeeze | solution.py:18
  111.8 2.9 %gather_fusion.11 = bf16[16,256,128]{2,1,0:T(8,128)(2,1)} fusion(bf16[256,16,128]{2,0,1:T(8,128)(2,1)} %copy.161, s32[1024]{0:T(1024)S(1)} %pad_clamp_fusion.2), kind=kCustom, calls=%fused_computation.2.clone | custom fusion | bytes 2097216 | tf_op jit(solution)/shard_map/jit(_take)/gather | solution.py:17
  114.7 2.8 %bitcast_convert_fusion = f32[256,16,128]{2,0,1:T(8,128)} fusion(bf16[16,256,128]{2,1,0:T(8,128)(2,1)} %gather_fusion.11, pred[16]{0:T(512)(128)(4,1)S(1)} %compare_and_fusion.1), kind=kLoop, calls=%fused_computation.38 | loop fusion | flops 1048576 | bytes 3145744 | tf_op jit(solution)/shard_map/convert_element_type | solution.py:30
  117.4 2.9 %copy.162 = f32[256,16,128]{0,2,1:T(8,128)} copy(f32[256,16,128]{2,0,1:T(8,128)} %bitcast_convert_fusion) | data formatting | bytes 4194304 | tf_op jit(solution)/shard_map/convert_element_type | solution.py:30
  120.3 4.1 %multiply_convert_fusion.2 = (bf16[256,8,128]{2,0,1:T(8,128)(2,1)}, bf16[256,8,128]{2,0,1:T(8,128)(2,1)S(1)}, bf16[256,8,128,1]{2,0,3,1:T(8,128)(2,1)S(1)}) fusion(f32[256,8,128]{2,0,1:T(8,128)} %convolution_bitcast_fusion.7, f32[256,8,128]{2,0,1:T(8,128)} %convolution_bitcast_fusion.6, bf16[2,8,2,128,128]{4,3,2,1,0:T(8,128)(2,1)} %param.17, ...), kind=kOutput, calls=%fused_computation.40 | convolution fusion | flops 139198464 | bytes 6292480 | tf_op jit(solution)/shard_map/rhkc,hkfc->rhf/dot_general | solution.py:31
  133.6 5.2 %scatter_fusion.1 = f32[256,16,128]{2,0,1:T(8,128)} fusion(f32[256,16,128]{2,0,1:T(8,128)} %broadcast.508.clone, s32[16]{0:T(128)S(1)} %fusion.49, f32[16,256,128]{2,1,0:T(8,128)} %bitcast.258), kind=kCustom, calls=%fused_computation.14 | custom fusion | flops 524288 | bytes 6291520 | tf_op jit(solution)/shard_map/scatter-add | solution.py:50
  138.9 2.9 %copy.166 = f32[256,16,128]{0,2,1:T(8,128)} copy(f32[256,16,128]{2,0,1:T(8,128)} %scatter_fusion.1) | data formatting | bytes 4194304 | tf_op jit(solution)/shard_map/scatter-add | solution.py:50
  141.8 3.5 %convolution_add_fusion.1 = f32[8,256,2,128]{3,1,2,0:T(8,128)} fusion(f32[8,256,2,128]{3,1,2,0:T(8,128)} %fusion.12, bf16[256,8,128,1]{2,0,3,1:T(8,128)(2,1)S(1)} %copy-done.16, bf16[2,8,2,128,128]{4,3,2,1,0:T(8,128)(2,1)} %param.16), kind=kOutput, calls=%fused_computation.25 | convolution fusion | flops 134742016 | bytes 5242880 | tf_op jit(solution)/shard_map/rhf,hkcf->rhkc/dot_general | solution.py:46
  146.9 5.0 %scatter_fusion = f32[256,16,128]{2,0,1:T(8,128)} fusion(f32[256,16,128]{2,0,1:T(8,128)} %broadcast.508.clone.1, s32[16]{0:T(128)S(1)} %fusion.47, f32[16,256,128]{2,1,0:T(8,128)} %bitcast.259), kind=kCustom, calls=%fused_computation.13 | custom fusion | flops 524288 | bytes 6291520 | tf_op jit(solution)/shard_map/scatter-add | solution.py:50
  151.9 2.9 %copy.158 = f32[256,16,128]{0,2,1:T(8,128)} copy(f32[256,16,128]{2,0,1:T(8,128)} %scatter_fusion) | data formatting | bytes 4194304 | tf_op jit(solution)/shard_map/scatter-add | solution.py:50
  154.9 4.5 %pad_maximum_fusion = f32[2,256,2048]{1,2,0:T(8,128)} fusion(f32[1,256,2048]{1,2,0:T(8,128)} %bitcast.265, f32[1,256,2048]{1,2,0:T(8,128)} %bitcast.266), kind=kLoop, calls=%fused_computation.16 | loop fusion | flops 1048576 | bytes 8388608 | tf_op jit(solution)/shard_map/stack | solution.py:135
  159.3 7.4 %copy.167 = f32[2,256,2048]{2,0,1:T(2,128)} copy(f32[2,256,2048]{1,2,0:T(8,128)} %pad_maximum_fusion) | data formatting | bytes 8388608 | tf_op jit(solution)/shard_map/stack | solution.py:135
  166.7 5.8 %all-to-all-start.2 = ((f32[2,256,2048]{2,0,1:T(2,128)}), f32[2,256,2048]{2,0,1:T(2,128)}, u32[]{:S(2)}, u32[]{:S(2)}) async-start(f32[2,256,2048]{2,0,1:T(2,128)} %copy.167), calls=%async_computation.2 | async-start | bytes 8388608 | tf_op jit(solution)/shard_map/all_to_all | solution.py:146
  180.1 2.5 %sort.17 = (s32[128]{0:T(128)}, s32[128]{0:T(128)S(1)}) sort(s32[128]{0:T(128)S(1)} %add.325, s32[128]{0:T(128)S(1)} %iota.56), dimensions={0}, to_apply=%region_8.10 | sort | flops 896 | bytes 2048 | tf_op jit(solution)/shard_map/jit(argsort)/sort | solution.py:103
  189.0 2.9 %copy.176 = f32[2,8,2,128,128]{4,3,2,1,0:T(8,128)} copy(f32[2,8,2,128,128]{3,4,2,1,0:T(8,128)} %pad_maximum_fusion.3) | data formatting | bytes 4194304
  196.4 29.4 %psum.7 = f32[2,256]{1,0:T(2,128)S(1)} all-reduce(f32[2,256]{1,0:T(2,128)S(1)} %pad_maximum_fusion.4), channel_id=1, replica_groups=mesh['expert'=16,'dp'=8] {'dp'}, use_global_device_ids=true, to_apply=%region_11.13 | all-reduce | flops 512 | bytes 4096 | tf_op jit(solution)/shard_map/psum | solution.py:140
  235.4 4.7 %reduce = f32[16,2,2,2048]{3,1,2,0:T(2,128)S(1)} reduce(f32[16,8,2,2,2048]{4,2,3,1,0:T(2,128)} %bitcast.74, f32[]{:T(128)} %constant.65.clone.1), dimensions={1}, to_apply=%region_6.8 | reduce | flops 917504 | bytes 4718596
  241.7 2.5 %scatter_custom_fusion.2 = f32[256,2048]{1,0:T(8,128)S(1)} fusion(s32[64]{0:T(128)S(1)} %fusion.46, f32[]{:T(128)} %constant.65.clone.1, f32[64,2048]{1,0:T(8,128)} %reshape.532, pred[64]{0:T(512)(128)(4,1)S(1)} %lt.230), kind=kCustom, calls=%fused_computation.50 | custom fusion | flops 262144 | bytes 2622976 | tf_op jit(solution)/shard_map/scatter-add | solution.py:154
  (179 shorter events, 67.8 us)
Async XLA Ops:
  0.6 2.5 %copy-start = (bf16[256,2048]{1,0:T(8,128)(2,1)S(1)}, bf16[256,2048]{1,0:T(8,128)(2,1)}, u32[]{:S(2)}) copy-start(bf16[256,2048]{1,0:T(8,128)(2,1)} %param.11) | copy-start | bytes 3145732
  0.6 1.3 copy-start.2
  2.8 1.3 copy-start.11
  9.0 11.2 %copy-start.25 = (s32[2,8,2]{1,2,0:T(2,128)S(1)}, s32[2,8,2]{1,2,0:T(2,128)}, u32[]{:S(2)}) copy-start(s32[2,8,2]{1,2,0:T(2,128)} %param.18) | copy-start | bytes 388
  9.0 13.7 %copy-start.26 = (s32[2,8,2]{1,2,0:T(2,128)S(1)}, s32[2,8,2]{1,2,0:T(2,128)}, u32[]{:S(2)}) copy-start(s32[2,8,2]{1,2,0:T(2,128)} %param.19) | copy-start | bytes 388
  9.0 15.0 %copy-start.3 = (f32[2,128]{1,0:T(2,128)S(1)}, f32[2,128]{1,0:T(2,128)}, u32[]{:S(2)}) copy-start(f32[2,128]{1,0:T(2,128)} %param.13) | copy-start | bytes 3076
  9.0 41.5 %all-to-all-start.1 = ((bf16[128,2,2,2048]{3,2,1,0:T(2,128)(2,1)}), bf16[128,2,2,2048]{3,2,1,0:T(2,128)(2,1)S(1)}, u32[]{:S(2)}, u32[]{:S(2)}) async-start(bf16[128,2,2,2048]{3,2,1,0:T(2,128)(2,1)} %bitcast.263), calls=%async_computation.1 | async-start | bytes 4194304 | tf_op jit(solution)/shard_map/all_to_all | solution.py:91
  53.9 35.7 %all-to-all-start = ((bf16[128,2,2,2048]{3,2,1,0:T(2,128)(2,1)}), bf16[128,2,2,2048]{3,2,1,0:T(2,128)(2,1)}, u32[]{:S(2)}, u32[]{:S(2)}) async-start(bf16[128,2,2,2048]{3,2,1,0:T(2,128)(2,1)} %bitcast.264), calls=%async_computation | async-start | bytes 4194304 | tf_op jit(solution)/shard_map/all_to_all | solution.py:92
  71.4 1.2 copy-start.12
  71.4 2.6 %copy-start.8 = (bf16[2,8,2,128,128]{4,3,2,1,0:T(8,128)(2,1)S(1)}, bf16[2,8,2,128,128]{4,3,2,1,0:T(8,128)(2,1)}, u32[]{:S(2)}) copy-start(bf16[2,8,2,128,128]{4,3,2,1,0:T(8,128)(2,1)} %param.16) | copy-start | bytes 3145732
  72.7 2.8 %copy-start.10 = (bf16[16,256,128]{2,1,0:T(8,128)(2,1)S(1)}, bf16[16,256,128]{2,1,0:T(8,128)(2,1)}, u32[]{:S(2)}) copy-start(bf16[16,256,128]{2,1,0:T(8,128)(2,1)} %gather_fusion.12) | copy-start | bytes 3145732
  120.3 4.1 %copy-start.13 = (bf16[2,8,2,128,128]{4,3,2,1,0:T(8,128)(2,1)S(1)}, bf16[2,8,2,128,128]{4,3,2,1,0:T(8,128)(2,1)}, u32[]{:S(2)}) copy-start(bf16[2,8,2,128,128]{4,3,2,1,0:T(8,128)(2,1)} %param.15) | copy-start | bytes 3145732
  120.3 4.6 %copy-start.23 = (f32[256,8,128]{2,0,1:T(8,128)S(1)}, f32[256,8,128]{2,0,1:T(8,128)}, u32[]{:S(2)}) copy-start(f32[256,8,128]{2,0,1:T(8,128)} %convolution_bitcast_fusion.9) | copy-start | bytes 3145732
  120.3 4.6 %copy-start.24 = (f32[256,8,128]{2,0,1:T(8,128)S(1)}, f32[256,8,128]{2,0,1:T(8,128)}, u32[]{:S(2)}) copy-start(f32[256,8,128]{2,0,1:T(8,128)} %convolution_bitcast_fusion.10) | copy-start | bytes 3145732
  124.4 4.1 %copy-start.17 = (bf16[256,8,128]{2,0,1:T(8,128)(2,1)}, bf16[256,8,128]{2,0,1:T(8,128)(2,1)S(1)}, u32[]{:S(2)}) copy-start(bf16[256,8,128]{2,0,1:T(8,128)(2,1)S(1)} %get-tuple-element.48) | copy-start | bytes 1572868
  124.4 5.9 %copy-start.14 = (bf16[256,8,128,1]{2,0,3,1:T(8,128)(2,1)}, bf16[256,8,128,1]{2,0,3,1:T(8,128)(2,1)S(1)}, u32[]{:S(2)}) copy-start(bf16[256,8,128,1]{2,0,3,1:T(8,128)(2,1)S(1)} %get-tuple-element.49) | copy-start | bytes 1572868
  124.4 2.0 copy-start.4
  124.4 2.2 copy-start.22
  128.5 3.6 %copy-start.19 = (bf16[256,8,128]{2,0,1:T(8,128)(2,1)}, bf16[256,8,128]{2,0,1:T(8,128)(2,1)S(1)}, u32[]{:S(2)}) copy-start(bf16[256,8,128]{2,0,1:T(8,128)(2,1)S(1)} %get-tuple-element.45) | copy-start | bytes 1572868
  128.5 1.8 copy-start.9
  138.9 2.9 %copy-start.16 = (bf16[256,8,128,1]{2,0,3,1:T(8,128)(2,1)S(1)}, bf16[256,8,128,1]{2,0,3,1:T(8,128)(2,1)}, u32[]{:S(2)}) copy-start(bf16[256,8,128,1]{2,0,3,1:T(8,128)(2,1)} %get-tuple-element.46) | copy-start | bytes 1572868
  166.7 68.6 %all-to-all-start.2 = ((f32[2,256,2048]{2,0,1:T(2,128)}), f32[2,256,2048]{2,0,1:T(2,128)}, u32[]{:S(2)}, u32[]{:S(2)}) async-start(f32[2,256,2048]{2,0,1:T(2,128)} %copy.167), calls=%async_computation.2 | async-start | bytes 8388608 | tf_op jit(solution)/shard_map/all_to_all | solution.py:146
  184.5 2.4 copy-start.6
  184.6 2.5 copy-start.20
  191.9 1.9 copy-start.5
  193.8 1.0 copy-start.21
  194.3 1.6 copy-start.7
  228.3 3.2 %copy-start.18 = (bf16[256,8,128]{2,0,1:T(8,128)(2,1)S(1)}, bf16[256,8,128]{2,0,1:T(8,128)(2,1)}, u32[]{:S(2)}) copy-start(bf16[256,8,128]{2,0,1:T(8,128)(2,1)} %copy-done.17) | copy-start | bytes 1572868
  229.9 2.1 copy-start.15
  241.7 3.7 %copy-start.1 = (bf16[256,2048]{1,0:T(8,128)(2,1)S(1)}, bf16[256,2048]{1,0:T(8,128)(2,1)}, u32[]{:S(2)}) copy-start(bf16[256,2048]{1,0:T(8,128)(2,1)} %param.11) | copy-start | bytes 3145732
where the time goes:
time: 247 us; the launch traced here: 245 us
  local copies, waits for them, and re-layouts  91.5 us (37%)
  other arithmetic  39.5 us (16%)
  waiting for transfers between devices  32.7 us (13%)
  blocking collectives  29.4 us (12%)
  matrix products  28.1 us (11%)
  starting transfers between devices  22.9 us (9%)
    psum x1, blocking collectives, on_device(): score_whole = lax.psum(score_parts, 'dp')  29.4 us
    all_to_all x1, waiting for transfers between devices, on_device(): lax.all_to_all(copies(sent_in), ('expert', 'dp'), split_axis=0, concat_ax...  21.5 us
    all_to_all x1, waiting for transfers between devices, on_device(): lax.all_to_all(copies(sent_grad), ('expert', 'dp'), split_axis=0, concat_...  11.2 us
    all_to_all x1, starting transfers between devices, on_device(): lax.all_to_all(copies(sent_in), ('expert', 'dp'), split_axis=0, concat_ax...  11.1 us
    scatter-add x2, other arithmetic, expert_part(): input_grad.at[:, in_blocks.reshape(-1)]  10.3 us
    another operation x4, local copies, waits for them, and re-layouts, expert_part(): rows_grad.reshape(row_count, block_count, block_size)  9.95 us
    unnamed x57, local copies, waits for them, and re-layouts  7.55 us
    another operation x1, local copies, waits for them, and re-layouts, on_device(): partial_grad = jnp.stack([outcome[0] for outcome in results])  7.38 us
  transfers between devices with their start and end apart: 3, of which 2 were waited for; matrix products, arithmetic and copies ran while one was open for 24% of the time, Pallas kernels for 0%

commit v1 on v0

v1 whole, which is shorter than its diff:
```python
import functools

import jax
import jax.numpy as jnp
from jax import lax
from jax.experimental import pallas as pl
from jax.experimental.pallas import tpu as pltpu
from jax.sharding import PartitionSpec as P

MESH = pl.DeviceIdType.MESH
BF, F32, I32 = jnp.bfloat16, jnp.float32, jnp.int32
RING = 4


def iota(shape, dim):
    return lax.broadcasted_iota(I32, shape, dim)


def as_bf(mask):
    return jnp.where(mask, 1.0, 0.0).astype(BF)


def dot(a, b, dims=((1,), (0,))):
    return lax.dot_general(a, b, (dims, ((), ())), preferred_element_type=F32)


def same_int(a, b):
    return -(((a - b) * (a - b) - 1) >> 31)


def log2(n):
    return n.bit_length() - 1


def exchange(
    dims, chosen_ref, scores_ref, grows_ref, dcols_ref, tokens_hbm, grads_hbm, gate_hbm, up_hbm, down_hbm,
    xg_out, h_out, a_out, u_out, back_out, scol_out, hot_out, gs_out,
    tok_v, grd_v, gate_v, up_v, down_v, base_v, slot_v, gsum_v, terms_v, h_v, a_v, u_v, gsx_send, gsx_recv,
    send1_0, send1_1, recv1_0, recv1_1, gath_0, gath_1, part_0, part_1, sib_0, sib_1,
    hop_send, hop_recv, fst_v, send2, back_0, back_1,
    load_sem, out_sem, p1_send, p1_recv, ag_send, ag_recv, sib_send, sib_recv, rs_send, rs_recv,
    p2_send, p2_recv, gs_send, gs_recv,
):
    G, M, D, T, HB = dims
    E2 = 2 * G
    SR = 2 * G
    Q, O = D // 4, D // 8
    NB = D // 128
    send1, recv1 = (send1_0, send1_1), (recv1_0, recv1_1)
    gath, part, sib, back = (gath_0, gath_1), (part_0, part_1), (sib_0, sib_1), (back_0, back_1)

    e, d = lax.axis_index("expert"), lax.axis_index("dp")
    x, c = d // 2, d % 2
    oc = 1 - c
    right = (e, ((x + 1) % RING) * 2 + c)
    left = (e, ((x + 3) % RING) * 2 + c)
    sibling = (e, x * 2 + oc)
    b_own = c * RING + x
    b_right = c * RING + (x + 1) % RING
    b_left = c * RING + (x + 3) % RING
    b_opp = c * RING + (x + 2) % RING

    loads = []
    for k, (src, dst) in enumerate(
        ((tokens_hbm, tok_v), (grads_hbm, grd_v), (gate_hbm, gate_v), (up_hbm, up_v), (down_hbm, down_v))
    ):
        cp = pltpu.make_async_copy(src, dst, load_sem.at[k])
        cp.start()
        loads.append(cp)

    barrier = pltpu.get_barrier_semaphore()

    @pl.loop(1, G)
    def _(i):
        pl.semaphore_signal(barrier, inc=1, device_id=((e + i) % G, d), device_id_type=MESH)

    @pl.loop(1, M)
    def _(i):
        pl.semaphore_signal(barrier, inc=1, device_id=(e, (d + i) % M), device_id_type=MESH)

    chosen = chosen_ref[...]
    cap = chosen.shape[1]
    lo = (e * M + d) * T
    pos = iota(chosen.shape, 1)
    before = jnp.sum(jnp.where(chosen < lo, 1, 0), axis=1, keepdims=True)
    count = jnp.sum(jnp.where(chosen < lo + T, 1, 0), axis=1, keepdims=True) - before
    tok_id = iota((E2, T), 1)
    for j in range(2):
        loc = jnp.sum(jnp.where(pos == before + j, chosen, 0), axis=1, keepdims=True) - lo
        loc = jnp.where(count > j, loc, -1)
        hot_out[j * E2 : (j + 1) * E2, :] = as_bf(tok_id == loc)
    owner = lax.shift_right_logical(chosen, log2(T))
    same = jnp.where((pltpu.roll(owner, 1, 1) == owner) & (pos > 0), 1, 0)
    member = owner & (M - 1)
    group = lax.shift_right_logical(owner, log2(M))
    slot_v[...] = ((member & 1) * RING + lax.shift_right_logical(member, 1)) * SR + group * 2 + same

    loads[0].wait()
    loads[1].wait()
    hot = hot_out[...]
    for arr, src in enumerate((tok_v, grd_v)):
        for q in range(4):
            base_v[arr * 4 + q] = dot(hot, src[:, q * Q : (q + 1) * Q]).astype(BF)

    def p1_copy(m, i):
        g = (e + i) % G
        return pltpu.make_async_remote_copy(
            src_ref=send1[m].at[g], dst_ref=recv1[m].at[e], send_sem=p1_send.at[m, i], recv_sem=p1_recv.at[m, i],
            device_id=(g, d), device_id_type=MESH,
        )

    def p2_copy(m, i):
        g = (e + i) % G
        return pltpu.make_async_remote_copy(
            src_ref=send2.at[m, g], dst_ref=back[m].at[e], send_sem=p2_send.at[m, i], recv_sem=p2_recv.at[m, i],
            device_id=(g, d), device_id_type=MESH,
        )

    stacked = base_v[...].reshape(8 * 2 * E2, Q)
    shape = (G * 16, 8 * 2 * E2)
    row, col = iota(shape, 0), iota(shape, 1)
    want = ((row >> 1) & 7) * (2 * E2) + (row & 1) * E2 + (row >> 4) * 2
    for m in range(2):
        send1[m][...] = dot(as_bf(col == want + m), stacked).astype(BF).reshape(G, 16, Q)
        if m == 0:
            pl.semaphore_wait(barrier, G - 1 + M - 1)
        recv1[m][e] = send1[m][e]

        @pl.loop(1, G)
        def _(i, m=m):
            p1_copy(m, i).start()

    def retile(m):
        @pl.loop(1, G)
        def _(i):
            p1_copy(m, i).wait_recv()

        shape = (16 * G, 16 * G)
        row, col = iota(shape, 0), iota(shape, 1)
        q = row >> log2(4 * G)
        arr = (row >> log2(2 * G)) & 1
        src = (row >> 1) & (G - 1)
        pick = as_bf(col == src * 16 + arr * 8 + q * 2 + (row & 1))
        out = dot(pick, recv1[m][...].reshape(16 * G, Q)).astype(BF)
        per_q = NB // 4
        for q in range(4):
            for i in range(per_q):
                gath[m][q * per_q + i, b_own] = out[q * 4 * G : (q + 1) * 4 * G, i * 128 : (i + 1) * 128]

    XR, GR = pl.ds(0, SR), pl.ds(SR, SR)

    def ag(m, k):
        b, rows, to = (
            (b_own, XR, right), (b_own, GR, right), (b_own, GR, left), (b_own, XR, left),
            (b_left, XR, right), (b_right, GR, left),
        )[k]
        ref = gath[m].at[:, b, rows]
        return pltpu.make_async_remote_copy(
            src_ref=ref, dst_ref=ref, send_sem=ag_send.at[m, k], recv_sem=ag_recv.at[m, k],
            device_id=to, device_id_type=MESH,
        )

    def sb(m, k):
        b, rows = (
            (b_own, XR), (b_own, GR), (b_left, XR), (b_left, GR), (b_right, GR), (b_right, XR), (b_opp, XR), (b_opp, GR),
        )[k]
        ref = gath[m].at[:, b, rows]
        return pltpu.make_async_remote_copy(
            src_ref=ref, dst_ref=ref, send_sem=sib_send.at[m, k], recv_sem=sib_recv.at[m, k],
            device_id=sibling, device_id_type=MESH,
        )

    def ag_start(m):
        for k in (0, 2, 1, 3):
            ag(m, k).start()
        sb(m, 0).start()
        sb(m, 1).start()

    def ag_relay(m):
        ag(m, 0).wait_recv()
        ag(m, 4).start()
        sb(m, 2).start()
        ag(m, 2).wait_recv()
        ag(m, 5).start()
        sb(m, 4).start()
        ag(m, 1).wait_recv()
        sb(m, 3).start()
        ag(m, 3).wait_recv()
        sb(m, 5).start()

    def ag_finish(m):
        ag(m, 4).wait_recv()
        sb(m, 6).start()
        ag(m, 5).wait_recv()
        sb(m, 7).start()
        for k in range(8):
            sb(m, k).wait_recv()
        pltpu.make_async_copy(gath[m], xg_out.at[m], out_sem.at[m, 0]).start()

    def weights(m, h):
        both = [
            jnp.concatenate([w[m, h, 0], w[m, h, 1]], axis=0) for w in (gate_v, up_v)
        ]
        return jnp.concatenate(both, axis=1)

    def picked(m, h, refs, lo_row):
        out = []
        for k in range(2):
            block = gath[m][refs[m, h, k], :, lo_row : lo_row + SR]
            out.append(block.reshape(M * SR, 128))
        return out

    def compute(m):
        mask = iota((M * SR, cap), 0) == slot_v[pl.ds(2 * e + m, 1), :]
        s = jnp.sum(jnp.where(mask, scores_ref[pl.ds(m, 1), :], 0.0), axis=1, keepdims=True)
        scol_out[m] = jnp.broadcast_to(s, (M * SR, 128))
        gsum_v[...] = jnp.zeros_like(gsum_v)

        @pl.loop(0, HB)
        def _(h):
            w = weights(m, h)
            ab = dot(jnp.concatenate(picked(m, h, grows_ref, 0), axis=1), w)
            a, b = ab[:, :128], ab[:, 128:]
            gk = picked(m, h, dcols_ref, SR)
            t = dot(gk[0], down_v[m, h, 0], ((1,), (1,))) + dot(gk[1], down_v[m, h, 1], ((1,), (1,)))
            sig = jax.nn.sigmoid(a)
            act = a * sig
            hid = (act * b).astype(BF)
            gsum_v[...] += hid.astype(F32) * t
            q = t * scol_out[m]
            ub = (q * act).astype(BF)
            ga = (q * b * sig * (1.0 + a * (1.0 - sig))).astype(BF)
            h_v[m, h] = hid
            a_v[m, h] = ga
            u_v[m, h] = ub
            r = dot(jnp.concatenate([ga, ub], axis=1), w, ((1,), (1,)))
            terms_v[2 * h] = r[:, :128]
            terms_v[2 * h + 1] = r[:, 128:]

        for k, (src, dst) in enumerate(((h_v, h_out), (a_v, a_out), (u_v, u_out))):
            pltpu.make_async_copy(src.at[m], dst.at[m], out_sem.at[m, k + 1]).start()
        total = jnp.sum(gsum_v[...], axis=1, keepdims=True)
        gsx_send[m : m + 1, :cap] = jnp.sum(jnp.where(mask, total, 0.0), axis=0, keepdims=True)

        @pl.loop(0, NB)
        def _(f):
            acc = jnp.zeros((M * SR, 128), F32)
            for h in range(HB):
                n0 = same_int(grows_ref[m, h, 0], f)
                n1 = (1 - n0) * same_int(grows_ref[m, h, 1], f)
                acc += terms_v[2 * HB - n0 * (2 * HB - 2 * h) - n1 * (2 * HB - 2 * h - 1)]
            part[m][:, :, pl.ds(pl.multiple_of(f * 128, 128), 128)] = acc.astype(BF).reshape(M, SR, 128)

        core_copy(m).start()

    def core_copy(m):
        return pltpu.make_async_remote_copy(
            src_ref=part[m].at[pl.ds(oc * RING, RING)], dst_ref=sib[m], send_sem=sib_send.at[m, 8],
            recv_sem=sib_recv.at[m, 8], device_id=sibling, device_id_type=MESH,
        )

    HA, HBH = slice(0, D // 2), slice(D // 2, D)

    def rs_copy(m, k):
        return pltpu.make_async_remote_copy(
            src_ref=hop_send.at[m, k], dst_ref=hop_recv.at[m, k], send_sem=rs_send.at[m, k],
            recv_sem=rs_recv.at[m, k], device_id=left if k % 2 else right, device_id_type=MESH,
        )

    def pair_sum(m, step, lanes):
        xx = (x + step) % RING
        return part[m][c * RING + xx, :, lanes].astype(F32) + sib[m][xx, :, lanes].astype(F32)

    def rs_start(m):
        core_copy(m).wait_recv()
        for k, step, lanes in ((0, 2, HA), (1, 2, HBH), (2, 1, HBH), (3, 3, HA)):
            hop_send[m, k] = pair_sum(m, step, lanes).astype(BF)
            rs_copy(m, k).start()

    def rs_middle(m):
        for k, step, lanes in ((4, 1, HA), (5, 3, HBH)):
            rs_copy(m, k - 4).wait_recv()
            hop_send[m, k] = (pair_sum(m, step, lanes) + hop_recv[m, k - 4].astype(F32)).astype(BF)
            rs_copy(m, k).start()

    def rs_finish(m):
        for k in (2, 3, 4, 5):
            rs_copy(m, k).wait_recv()
        fin_a = pair_sum(m, 0, HA) + hop_recv[m, 4].astype(F32) + hop_recv[m, 3].astype(F32)
        fin_b = pair_sum(m, 0, HBH) + hop_recv[m, 2].astype(F32) + hop_recv[m, 5].astype(F32)
        for o in range(4):
            fst_v[o] = fin_a[:, o * O : (o + 1) * O].astype(BF)
            fst_v[o + 4] = fin_b[:, o * O : (o + 1) * O].astype(BF)
        shape = (16 * G, 8 * SR)
        row, col = iota(shape, 0), iota(shape, 1)
        pick = as_bf(col == ((row >> 1) & 7) * SR + (row >> 4) * 2 + (row & 1))
        send2[m] = dot(pick, fst_v[...].reshape(8 * SR, O)).astype(BF).reshape(G, 16, O)
        back[m][e] = send2[m, e]

        @pl.loop(1, G)
        def _(i):
            p2_copy(m, i).start()

    def return_finish(m):
        @pl.loop(1, G)
        def _(i):
            p2_copy(m, i).wait_recv()

        pltpu.make_async_copy(back[m], back_out.at[m], out_sem.at[m, 4]).start()

    def gs_copy(i):
        return pltpu.make_async_remote_copy(
            src_ref=gsx_send, dst_ref=gsx_recv.at[d], send_sem=gs_send.at[i], recv_sem=gs_recv.at[i],
            device_id=(e, (d + i) % M), device_id_type=MESH,
        )

    terms_v[2 * HB] = jnp.zeros((M * SR, 128), F32)
    gsx_send[...] = jnp.zeros_like(gsx_send)
    retile(0)
    ag_start(0)
    retile(1)
    ag_relay(0)
    ag_start(1)
    ag_finish(0)
    for cp in loads[2:]:
        cp.wait()
    compute(0)
    ag_relay(1)
    rs_start(0)
    ag_finish(1)
    rs_middle(0)
    compute(1)
    gsx_recv[d] = gsx_send[...]

    @pl.loop(1, M)
    def _(i):
        gs_copy(i).start()

    rs_finish(0)
    rs_start(1)
    rs_middle(1)
    return_finish(0)
    rs_finish(1)

    @pl.loop(1, M)
    def _(i):
        gs_copy(i).wait_recv()

    gs = gsx_recv[0]
    for i in range(1, M):
        gs = gs + gsx_recv[i]
    gs_out[...] = gs[:2, :cap]
    return_finish(1)

    for m in range(2):

        @pl.loop(1, G)
        def _(i, m=m):
            p1_copy(m, i).wait_send()
            p2_copy(m, i).wait_send()

        for k in range(6):
            ag(m, k).wait_send()
            rs_copy(m, k).wait_send()
        for k in range(8):
            sb(m, k).wait_send()
        core_copy(m).wait_send()
        for k, (src, dst) in enumerate(
            ((gath[m], xg_out), (h_v.at[m], h_out), (a_v.at[m], a_out), (u_v.at[m], u_out), (back[m], back_out))
        ):
            pltpu.make_async_copy(src, dst.at[m], out_sem.at[m, k]).wait()

    @pl.loop(1, M)
    def _(i):
        gs_copy(i).wait_send()


def block_grads(
    dims, per_step, grows_ref, dcols_ref, xg_ref, h_ref, a_ref, u_ref, back_ref, scol_ref, hot_ref,
    gt_ref, gg_ref, gu_ref, gd_ref,
):
    G, M, D, T, HB = dims
    E2, SR, O = 2 * G, 2 * G, D // 8
    m, step = pl.program_id(0), pl.program_id(1)

    def picked(h, refs, lo_row):
        out = []
        for k in range(2):
            out.append(xg_ref[0, refs[m, h, k], :, lo_row : lo_row + SR].reshape(M * SR, 128))
        return out

    for i in range(per_step):
        h = step * per_step + i
        xx = jnp.concatenate(picked(h, grows_ref, 0), axis=1)
        au = jnp.concatenate([a_ref[0, i], u_ref[0, i]], axis=1)
        both = dot(xx, au, ((0,), (0,)))
        scol = scol_ref[0]
        pp = jnp.concatenate([(g.astype(F32) * scol).astype(BF) for g in picked(h, dcols_ref, SR)], axis=1)
        down = dot(h_ref[0, i], pp, ((0,), (0,)))
        for k in range(2):
            gg_ref[0, i, k] = both[k * 128 : (k + 1) * 128, :128]
            gu_ref[0, i, k] = both[k * 128 : (k + 1) * 128, 128:]
            gd_ref[0, i, k] = down[:, k * 128 : (k + 1) * 128]

    @pl.when((m == 0) & (step == 0))
    def _():
        shape = (8 * 2 * E2, 2 * 16 * G)
        row, col = iota(shape, 0), iota(shape, 1)
        o, j = row >> log2(2 * E2), (row >> log2(E2)) & 1
        g, mm = (row >> 1) & (G - 1), row & 1
        pick = as_bf(col == mm * (16 * G) + g * 16 + o * 2 + j)
        vals = dot(pick, back_ref[...].reshape(2 * 16 * G, O)).astype(BF)
        for o in range(8):
            block = vals[o * 2 * E2 : (o + 1) * 2 * E2]
            gt_ref[:, o * O : (o + 1) * O] = dot(hot_ref[...], block, ((0,), (0,))).astype(BF)


def on_device(tokens, grad_out, scores, chosen, gate_vals, up_vals, down_vals, gate_rows, down_cols):
    G, M = lax.axis_size("expert"), lax.axis_size("dp")
    T, D = tokens.shape
    HB = gate_vals.shape[1]
    cap = chosen.shape[1]
    dims = (G, M, D, T, HB)
    SR, O, Q = 2 * G, D // 8, D // 4
    rows = M * SR
    hbm, vmem, smem = (pl.BlockSpec(memory_space=s) for s in (pl.ANY, pltpu.VMEM, pltpu.SMEM))
    dma = pltpu.SemaphoreType.DMA
    sds = jax.ShapeDtypeStruct
    xg, hid, ga, ub, back, scol, hot, gs = pl.pallas_call(
        functools.partial(exchange, dims),
        out_shape=(
            sds((2, D // 128, M, 2 * SR, 128), BF),
            sds((2, HB, rows, 128), BF),
            sds((2, HB, rows, 128), BF),
            sds((2, HB, rows, 128), BF),
            sds((2, G, 16, O), BF),
            sds((2, rows, 128), F32),
            sds((4 * G, T), BF),
            sds((2, cap), F32),
        ),
        in_specs=[vmem, vmem, smem, smem] + [hbm] * 5,
        out_specs=(hbm,) * 5 + (vmem,) * 3,
        scratch_shapes=[
            pltpu.VMEM((T, D), BF),
            pltpu.VMEM((T, D), BF),
            pltpu.VMEM(gate_vals.shape, BF),
            pltpu.VMEM(gate_vals.shape, BF),
            pltpu.VMEM(gate_vals.shape, BF),
            pltpu.VMEM((8, 4 * G, Q), BF),
            pltpu.VMEM(chosen.shape, I32),
            pltpu.VMEM((rows, 128), F32),
            pltpu.VMEM((2 * HB + 1, rows, 128), F32),
            pltpu.VMEM((2, HB, rows, 128), BF),
            pltpu.VMEM((2, HB, rows, 128), BF),
            pltpu.VMEM((2, HB, rows, 128), BF),
            pltpu.VMEM((8, 128), F32),
            pltpu.VMEM((M, 8, 128), F32),
            pltpu.VMEM((G, 16, Q), BF),
            pltpu.VMEM((G, 16, Q), BF),
            pltpu.VMEM((G, 16, Q), BF),
            pltpu.VMEM((G, 16, Q), BF),
            pltpu.VMEM((D // 128, M, 2 * SR, 128), BF),
            pltpu.VMEM((D // 128, M, 2 * SR, 128), BF),
            pltpu.VMEM((M, SR, D), BF),
            pltpu.VMEM((M, SR, D), BF),
            pltpu.VMEM((RING, SR, D), BF),
            pltpu.VMEM((RING, SR, D), BF),
            pltpu.VMEM((2, 6, SR, D // 2), BF),
            pltpu.VMEM((2, 6, SR, D // 2), BF),
            pltpu.VMEM((8, SR, O), BF),
            pltpu.VMEM((2, G, 16, O), BF),
            pltpu.VMEM((G, 16, O), BF),
            pltpu.VMEM((G, 16, O), BF),
            dma((5,)),
            dma((2, 5)),
            dma((2, G)),
            dma((2, G)),
            dma((2, 6)),
            dma((2, 6)),
            dma((2, 9)),
            dma((2, 9)),
            dma((2, 6)),
            dma((2, 6)),
            dma((2, G)),
            dma((2, G)),
            dma((M,)),
            dma((M,)),
        ],
        compiler_params=pltpu.CompilerParams(
            collective_id=0, has_side_effects=True, vmem_limit_bytes=44 * 1024 * 1024
        ),
        name="exchange",
    )(chosen, scores, gate_rows, down_cols, tokens, grad_out, gate_vals, up_vals, down_vals)

    per_step = 2
    spec = pl.BlockSpec

    def by_step(*tail):
        return spec((1, per_step) + tail, lambda m, i, *_: (m, i) + (0,) * len(tail))

    def by_member(*tail):
        return spec((1,) + tail, lambda m, i, *_: (m,) + (0,) * len(tail))

    def whole(*shape):
        return spec(shape, lambda m, i, *_: (0,) * len(shape))

    grads = sds(gate_vals.shape, F32)
    grad_tokens, grad_gate, grad_up, grad_down = pl.pallas_call(
        functools.partial(block_grads, dims, per_step),
        out_shape=(sds((T, D), BF), grads, grads, grads),
        grid_spec=pltpu.PrefetchScalarGridSpec(
            num_scalar_prefetch=2,
            grid=(2, HB // per_step),
            in_specs=[
                by_member(D // 128, M, 2 * SR, 128),
                by_step(rows, 128),
                by_step(rows, 128),
                by_step(rows, 128),
                whole(2, G, 16, O),
                by_member(rows, 128),
                whole(4 * G, T),
            ],
            out_specs=(
                whole(T, D),
                by_step(2, 128, 128),
                by_step(2, 128, 128),
                by_step(2, 128, 128),
            ),
        ),
        compiler_params=pltpu.CompilerParams(vmem_limit_bytes=40 * 1024 * 1024),
        name="block_grads",
    )(gate_rows, down_cols, xg, hid, ga, ub, back, scol, hot)
    return grad_tokens, grad_gate, grad_up, grad_down, gs


def solution(mesh):
    rows = P(("expert", "dp"), None)
    blocks = P("expert", "dp", None, None, None)
    links = P("expert", "dp", None)
    return jax.shard_map(
        on_device,
        mesh=mesh,
        in_specs=(rows, rows, P("expert", None), P(), blocks, blocks, blocks, links, links),
        out_specs=(rows, blocks, blocks, blocks, P("expert", None)),
        check_vma=False,
    )
```

time: 247 us -> 81.7 us (0.33)
  local copies, waits for them, and re-layouts: 91.5 us -> 11.8 us
  Pallas kernels: 0 us -> 68.4 us
  other arithmetic: 39.5 us -> 0 us
  waiting for transfers between devices: 32.7 us -> 0 us
  blocking collectives: 29.4 us -> 0 us
  matrix products: 28.1 us -> 0 us
  starting transfers between devices: 22.9 us -> 0 us
    pallas_call x0 -> x2, Pallas kernels: none -> 68.4 us  [the longest x1 61.3 us: on_device(): pl.pallas_call(functools.partial(exchange, dims), out_shape=(sds((2, D //...]
    all_to_all x3 -> x0, waiting for transfers between devices: 32.7 us -> none  [the longest x1 21.5 us: on_device(): lax.all_to_all(copies(sent_in), ('expert', 'dp'), split_axis=0, concat_ax...]
    psum x1 -> x0, blocking collectives: 29.4 us -> none  [on_device(): score_whole = lax.psum(score_parts, 'dp')]
    dot_general x16 -> x0, matrix products: 25.9 us -> none  [the longest x2 5.97 us: expert_part(): jnp.einsum('rhkc,hkfc->rhf', scaled, down_block, preferred_element_type=j...]
    another operation x17 -> x0, local copies, waits for them, and re-layouts: 25.9 us -> none  [the longest x4 9.95 us: expert_part(): rows_grad.reshape(row_count, block_count, block_size)]
    gather x20 -> x0, local copies, waits for them, and re-layouts: 25.1 us -> none  [the longest x2 5.75 us: expert_part(): jnp.take(rows_grad.reshape(row_count, block_count, block_size), out_block...]
    all_to_all x3 -> x0, starting transfers between devices: 22.9 us -> none  [the longest x1 11.1 us: on_device(): lax.all_to_all(copies(sent_in), ('expert', 'dp'), split_axis=0, concat_ax...]
    scatter-add x3 -> x0, other arithmetic: 12.8 us -> none  [the longest x2 10.3 us: expert_part(): input_grad.at[:, in_blocks.reshape(-1)]]
  transfers between devices with their start and end apart: 3 -> 0, of which waited for: 2 -> 0; matrix products, arithmetic and copies ran while one was open for 24% -> 0% of each run, Pallas kernels for 0% -> 0%
where the time goes in v1:
time: 81.7 us; the launch traced here: 80.9 us
  Pallas kernels  68.4 us (84%)
  local copies, waits for them, and re-layouts  11.8 us (14%)
    pallas_call x1, Pallas kernels, on_device(): pl.pallas_call(functools.partial(exchange, dims), out_shape=(sds((2, D //...  61.3 us
    unnamed x19, local copies, waits for them, and re-layouts  11.8 us
    pallas_call x1, Pallas kernels, on_device(): pl.pallas_call(functools.partial(block_grads, dims, per_step), out_shape=...  7.12 us

profile of v1, /device:TPU:0, one launch (start us, length us, event | category | flops | bytes accessed | tf_op | source)
XLA Modules:
  0.0 80.9 jit_solution(8561739582384255198)
XLA Ops:
  0.6 0.8 copy.16.grows_ref
  1.4 0.8 copy.17.dcols_ref
  2.2 0.0 copy-start.1
  2.2 1.2 %copy-done.1 = bf16[256,2048]{1,0:T(8,128)(2,1)S(1)} copy-done((bf16[256,2048]{1,0:T(8,128)(2,1)S(1)}, bf16[256,2048]{1,0:T(8,128)(2,1)}, u32[]{:S(2)}) %copy-start.1) | copy-done | bytes 1048600
  3.4 0.0 copy-start.2
  3.4 1.2 %copy-done.2 = bf16[256,2048]{1,0:T(8,128)(2,1)S(1)} copy-done((bf16[256,2048]{1,0:T(8,128)(2,1)S(1)}, bf16[256,2048]{1,0:T(8,128)(2,1)}, u32[]{:S(2)}) %copy-start.2) | copy-done | bytes 1048600
  4.6 0.0 copy-start.3
  4.6 1.2 %copy-done.3 = bf16[2,8,2,128,128]{4,3,2,1,0:T(8,128)(2,1)S(1)} copy-done((bf16[2,8,2,128,128]{4,3,2,1,0:T(8,128)(2,1)S(1)}, bf16[2,8,2,128,128]{4,3,2,1,0:T(8,128)(2,1)}, u32[]{:S(2)}) %copy-start.3) | copy-done | bytes 1048600
  5.8 0.0 copy-start.4
  5.8 1.2 %copy-done.4 = bf16[2,8,2,128,128]{4,3,2,1,0:T(8,128)(2,1)S(1)} copy-done((bf16[2,8,2,128,128]{4,3,2,1,0:T(8,128)(2,1)S(1)}, bf16[2,8,2,128,128]{4,3,2,1,0:T(8,128)(2,1)}, u32[]{:S(2)}) %copy-start.4) | copy-done | bytes 1048600
  7.1 0.0 copy-start.5
  7.1 1.2 %copy-done.5 = bf16[2,8,2,128,128]{4,3,2,1,0:T(8,128)(2,1)S(1)} copy-done((bf16[2,8,2,128,128]{4,3,2,1,0:T(8,128)(2,1)S(1)}, bf16[2,8,2,128,128]{4,3,2,1,0:T(8,128)(2,1)}, u32[]{:S(2)}) %copy-start.5) | copy-done | bytes 1048600
  8.3 0.0 copy-start.6
  8.3 0.7 copy-done.6
  9.0 0.0 copy-start.7
  9.0 0.7 copy-done.7
  9.7 61.3 %exchange.1 = (bf16[2,16,8,64,128]{4,3,2,1,0:T(8,128)(2,1)}, bf16[2,8,256,128]{3,2,1,0:T(8,128)(2,1)S(1)}, bf16[2,8,256,128]{3,2,1,0:T(8,128)(2,1)S(1)}, bf16[2,...) custom-call(s32[32,128]{1,0:T(8,128)S(1)} %copy-done.6, ...), custom_call_target="tpu_custom_call" | custom-call | tf_op jit(solution)/shard_map/exchange/pallas_call | solution.py:429
  71.0 0.0 copy-start
  71.0 2.2 %copy-done = bf16[2,16,8,64,128]{4,3,2,1,0:T(8,128)(2,1)S(1)} copy-done((bf16[2,16,8,64,128]{4,3,2,1,0:T(8,128)(2,1)S(1)}, bf16[2,16,8,64,128]{4,3,2,1,0:T(8,128)(2,1)}, u32[]{:S(2)}) %copy-start) | copy-done | bytes 4194328
  73.2 7.1 %block_grads.1 = (bf16[256,2048]{1,0:T(8,128)(2,1)}, f32[2,8,2,128,128]{4,3,2,1,0:T(8,128)}, f32[2,8,2,128,128]{4,3,2,1,0:T(8,128)}, f32[2,8,2,128,128]{4,3,2,1,0:T(8,128)}) custom-call(s32[2,8,2]{2,1,0:T(8,128)S(1)} %copy.16.grows_ref, s32[2,8,2]{2,1,0:T(8,128)S(1)} %copy.17.dcols_ref, bf16[2,16,8,64,128]{4,3,2,1,0:T(8,128)(2,1)S(1)} %copy-done, ...), custom_call_target="tpu_custom_call" | custom-call | tf_op jit(solution)/shard_map/block_grads/pallas_call | solution.py:508
  80.3 0.6 copy.19
Async XLA Ops:
  2.2 1.2 %copy-start.1 = (bf16[256,2048]{1,0:T(8,128)(2,1)S(1)}, bf16[256,2048]{1,0:T(8,128)(2,1)}, u32[]{:S(2)}) copy-start(bf16[256,2048]{1,0:T(8,128)(2,1)} %tokens_hbm.1) | copy-start | bytes 3145732
  3.4 1.2 %copy-start.2 = (bf16[256,2048]{1,0:T(8,128)(2,1)S(1)}, bf16[256,2048]{1,0:T(8,128)(2,1)}, u32[]{:S(2)}) copy-start(bf16[256,2048]{1,0:T(8,128)(2,1)} %grads_hbm.1) | copy-start | bytes 3145732
  4.6 1.2 %copy-start.3 = (bf16[2,8,2,128,128]{4,3,2,1,0:T(8,128)(2,1)S(1)}, bf16[2,8,2,128,128]{4,3,2,1,0:T(8,128)(2,1)}, u32[]{:S(2)}) copy-start(bf16[2,8,2,128,128]{4,3,2,1,0:T(8,128)(2,1)} %gate_hbm.1) | copy-start | bytes 3145732
  5.8 1.2 %copy-start.4 = (bf16[2,8,2,128,128]{4,3,2,1,0:T(8,128)(2,1)S(1)}, bf16[2,8,2,128,128]{4,3,2,1,0:T(8,128)(2,1)}, u32[]{:S(2)}) copy-start(bf16[2,8,2,128,128]{4,3,2,1,0:T(8,128)(2,1)} %up_hbm.1) | copy-start | bytes 3145732
  7.1 1.2 %copy-start.5 = (bf16[2,8,2,128,128]{4,3,2,1,0:T(8,128)(2,1)S(1)}, bf16[2,8,2,128,128]{4,3,2,1,0:T(8,128)(2,1)}, u32[]{:S(2)}) copy-start(bf16[2,8,2,128,128]{4,3,2,1,0:T(8,128)(2,1)} %down_hbm.1) | copy-start | bytes 3145732
  8.3 0.7 copy-start.6
  9.0 0.7 copy-start.7
  71.0 2.2 %copy-start = (bf16[2,16,8,64,128]{4,3,2,1,0:T(8,128)(2,1)S(1)}, bf16[2,16,8,64,128]{4,3,2,1,0:T(8,128)(2,1)}, u32[]{:S(2)}) copy-start(bf16[2,16,8,64,128]{4,3,2,1,0:T(8,128)(2,1)} %get-tuple-element.17.xg_ref) | copy-start | bytes 12582916

commit v2 on v1

v2 whole, which is shorter than its diff:
```python
import functools

import jax
import jax.numpy as jnp
from jax import lax
from jax.experimental import pallas as pl
from jax.experimental.pallas import tpu as pltpu
from jax.sharding import PartitionSpec as P

MESH = pl.DeviceIdType.MESH
BF, F32, I32 = jnp.bfloat16, jnp.float32, jnp.int32
RING = 4


def iota(shape, dim):
    return lax.broadcasted_iota(I32, shape, dim)


def as_bf(mask):
    return jnp.where(mask, 1.0, 0.0).astype(BF)


def dot(a, b, dims=((1,), (0,))):
    return lax.dot_general(a, b, (dims, ((), ())), preferred_element_type=F32)


def same_int(a, b):
    return -(((a - b) * (a - b) - 1) >> 31)


def log2(n):
    return n.bit_length() - 1


def exchange(
    dims, chosen_hbm, scores_hbm, grows_hbm, dcols_hbm, tokens_hbm, grads_hbm, gate_hbm, up_hbm, down_hbm,
    gt_out, gg_out, gu_out, gd_out, gs_out,
    chosen_v, scores_v, grows_s, dcols_s, table_s, tok_v, grd_v, gate_v, up_v, down_v, wt_v, dt_v, hot_v, hotm_v, base_v,
    slot_v, scol_v, gsum_v, terms_v, h_v, a_v, u_v, p_v, gsx_send, gsx_recv, gt_v,
    send1_0, send1_1, recv1_0, recv1_1, gath_0, gath_1, part_0, part_1, own_0, own_1, sib_0, sib_1,
    hop_send, hop_recv, fst_v, send2, back_0, back_1,
    load_sem, p1_send, p1_recv, ag_send, ag_recv, sib_send, sib_recv, rs_send, rs_recv,
    p2_send, p2_recv, gs_send, gs_recv,
):
    G, M, D, T, HB = dims
    E2 = 2 * G
    SR = 2 * G
    Q, O = D // 4, D // 8
    NB = D // 128
    send1, recv1 = (send1_0, send1_1), (recv1_0, recv1_1)
    gath, part, own = (gath_0, gath_1), (part_0, part_1), (own_0, own_1)
    sib, back = (sib_0, sib_1), (back_0, back_1)

    e, d = lax.axis_index("expert"), lax.axis_index("dp")
    x, c = d // 2, d % 2
    oc = 1 - c
    right = (e, ((x + 1) % RING) * 2 + c)
    left = (e, ((x + 3) % RING) * 2 + c)
    sibling = (e, x * 2 + oc)
    b_own = c * RING + x
    b_right = c * RING + (x + 1) % RING
    b_left = c * RING + (x + 3) % RING
    b_opp = c * RING + (x + 2) % RING

    barrier = pltpu.get_barrier_semaphore()

    @pl.loop(1, G)
    def _(i):
        pl.semaphore_signal(barrier, inc=1, device_id=((e + i) % G, d), device_id_type=MESH)

    @pl.loop(1, M)
    def _(i):
        pl.semaphore_signal(barrier, inc=1, device_id=(e, (d + i) % M), device_id_type=MESH)

    loads = []
    for k, (src, dst) in enumerate((
        (chosen_hbm, chosen_v), (tokens_hbm, tok_v), (grads_hbm, grd_v), (scores_hbm, scores_v), (grows_hbm, grows_s),
        (dcols_hbm, dcols_s), (gate_hbm, gate_v), (up_hbm, up_v), (down_hbm, down_v),
    )):
        loads.append(pltpu.make_async_copy(src, dst, load_sem.at[k]))
    for cp in loads[:6]:
        cp.start()

    loads[0].wait()
    chosen = chosen_v[...]
    cap = chosen.shape[1]
    lo = (e * M + d) * T
    pos = iota(chosen.shape, 1)
    before = jnp.sum(jnp.where(chosen < lo, 1, 0), axis=1, keepdims=True)
    count = jnp.sum(jnp.where(chosen < lo + T, 1, 0), axis=1, keepdims=True) - before
    tok_id = iota((E2, T), 1)
    for j in range(2):
        loc = jnp.sum(jnp.where(pos == before + j, chosen, 0), axis=1, keepdims=True) - lo
        loc = jnp.where(count > j, loc, -1)
        hot_v[j * E2 : (j + 1) * E2, :] = as_bf(tok_id == loc)

    hot = hot_v[...]
    for arr, src in enumerate((tok_v, grd_v)):
        loads[1 + arr].wait()
        for q in range(4):
            base_v[arr * 4 + q] = dot(hot, src[:, q * Q : (q + 1) * Q]).astype(BF)

    arriving, leaving = {}, []

    def go(make, *key):
        make(*key).start()
        arriving[make, key] = lambda: make(*key).wait_recv()
        leaving.append(lambda: make(*key).wait_send())

    def go_all(make, n, *key):
        @pl.loop(1, n)
        def _(i):
            make(*key, i).start()

        def arrive():
            @pl.loop(1, n)
            def _(i):
                make(*key, i).wait_recv()

        def leave():
            @pl.loop(1, n)
            def _(i):
                make(*key, i).wait_send()

        arriving[make, key] = arrive
        leaving.append(leave)

    def got(make, *key):
        arriving.pop((make, key))()

    def p1_copy(m, i):
        g = (e + i) % G
        return pltpu.make_async_remote_copy(
            src_ref=send1[m].at[g], dst_ref=recv1[m].at[e], send_sem=p1_send.at[m, i], recv_sem=p1_recv.at[m, i],
            device_id=(g, d), device_id_type=MESH,
        )

    def p2_copy(m, i):
        g = (e + i) % G
        return pltpu.make_async_remote_copy(
            src_ref=send2.at[m, g], dst_ref=back[m].at[e], send_sem=p2_send.at[m, i], recv_sem=p2_recv.at[m, i],
            device_id=(g, d), device_id_type=MESH,
        )

    stacked = base_v[...].reshape(8 * 2 * E2, Q)
    shape = (G * 16, 8 * 2 * E2)
    row, col = iota(shape, 0), iota(shape, 1)
    want = ((row >> 1) & 7) * (2 * E2) + (row & 1) * E2 + (row >> 4) * 2
    for m in range(2):
        send1[m][...] = dot(as_bf(col == want + m), stacked).astype(BF).reshape(G, 16, Q)
        if m == 0:
            pl.semaphore_wait(barrier, G - 1 + M - 1)
        go_all(p1_copy, G, m)
        recv1[m][e] = send1[m][e]
    for cp in loads[6:]:
        cp.start()

    def prepare():
        owner = lax.shift_right_logical(chosen, log2(T))
        same = jnp.where((pltpu.roll(owner, 1, 1) == owner) & (pos > 0), 1, 0)
        member = owner & (M - 1)
        group = lax.shift_right_logical(owner, log2(M))
        slot_v[...] = ((member & 1) * RING + lax.shift_right_logical(member, 1)) * SR + group * 2 + same
        for cp in loads[3:6]:
            cp.wait()
        for m in range(2):
            s = jnp.sum(jnp.where(slot_mask(m), scores_v[m : m + 1, :], 0.0), axis=1, keepdims=True)
            scol_v[m] = jnp.broadcast_to(s, (M * SR, 128)).reshape(M, SR, 128)
            row, col = iota((E2, 2 * E2), 0), iota((E2, 2 * E2), 1)
            pick = as_bf(col == (row >> log2(G)) * E2 + (row & (G - 1)) * 2 + m)
            hotm_v[m] = dot(pick, hot_v[...]).astype(BF)

        @pl.loop(0, 2 * HB)
        def _(i):
            m, h = i // HB, i % HB
            g0, g1 = grows_s[m, 0, h], grows_s[m, 1, h]
            for f in range(NB):
                n0 = same_int(g0, f)
                n1 = (1 - n0) * same_int(g1, f)
                table_s[i * NB + f] = 2 * HB - n0 * (2 * HB - 2 * h) - n1 * (2 * HB - 2 * h - 1)

        for cp in loads[6:]:
            cp.wait()

        @pl.loop(0, 2 * HB)
        def _(i):
            m, h = i // HB, i % HB
            for k in range(2):
                span = slice(k * 128, (k + 1) * 128)
                wt_v[m, h, :128, span] = gate_v[m, h, k].T
                wt_v[m, h, 128:, span] = up_v[m, h, k].T
                dt_v[m, h, span, :] = down_v[m, h, k].T

        terms_v[2 * HB] = jnp.zeros((2, M // 2 * SR, 128), F32)
        gsx_send[...] = jnp.zeros_like(gsx_send)

    def slot_mask(m):
        return iota((M * SR, cap), 0) == slot_v[pl.ds(2 * e + m, 1), :]

    def retile(m):
        got(p1_copy, m)
        shape = (16 * G, 16 * G)
        row, col = iota(shape, 0), iota(shape, 1)
        q = row >> log2(4 * G)
        arr = (row >> log2(2 * G)) & 1
        src = (row >> 1) & (G - 1)
        pick = as_bf(col == src * 16 + arr * 8 + q * 2 + (row & 1))
        out = dot(pick, recv1[m][...].reshape(16 * G, Q)).astype(BF)
        per_q = NB // 4
        for q in range(4):
            for i in range(per_q):
                gath[m][q * per_q + i, b_own] = out[q * 4 * G : (q + 1) * 4 * G, i * 128 : (i + 1) * 128]

    XR, GR = pl.ds(0, SR), pl.ds(SR, SR)

    def ag(m, k):
        b, rows, to = (
            (b_own, XR, right), (b_own, GR, right), (b_own, GR, left), (b_own, XR, left),
            (b_left, XR, right), (b_right, GR, left),
        )[k]
        ref = gath[m].at[:, b, rows]
        return pltpu.make_async_remote_copy(
            src_ref=ref, dst_ref=ref, send_sem=ag_send.at[m, k], recv_sem=ag_recv.at[m, k],
            device_id=to, device_id_type=MESH,
        )

    def sb(m, k):
        b, rows = (
            (b_own, XR), (b_own, GR), (b_left, XR), (b_left, GR), (b_right, GR), (b_right, XR), (b_opp, XR), (b_opp, GR),
        )[k]
        ref = gath[m].at[:, b, rows]
        return pltpu.make_async_remote_copy(
            src_ref=ref, dst_ref=ref, send_sem=sib_send.at[m, k], recv_sem=sib_recv.at[m, k],
            device_id=sibling, device_id_type=MESH,
        )

    def scale(m, blocks):
        for b in blocks:
            s = scol_v[m, b]
            for f in range(NB):
                p_v[m, f, b] = (gath[m][f, b, SR:].astype(F32) * s).astype(BF)

    def ag_start(m):
        for k in (0, 2, 1, 3):
            go(ag, m, k)
        go(sb, m, 0)
        go(sb, m, 1)

    def ag_relay(m):
        got(ag, m, 0)
        go(ag, m, 4)
        go(sb, m, 2)
        got(ag, m, 2)
        go(ag, m, 5)
        go(sb, m, 4)
        got(ag, m, 1)
        go(sb, m, 3)
        got(ag, m, 3)
        go(sb, m, 5)

    def ag_finish(m):
        scale(m, (b_own, b_left, b_right))
        got(ag, m, 4)
        go(sb, m, 6)
        got(ag, m, 5)
        go(sb, m, 7)
        for k in range(8):
            got(sb, m, k)
        scale(m, (b_opp,) + tuple(oc * RING + i for i in range(RING)))

    def picked_in(m, h):
        blocks = [gath[m][grows_s[m, k, h], :, :SR].reshape(M * SR, 128) for k in range(2)]
        return jnp.concatenate(blocks, axis=1)

    def picked_out(m, h):
        return jnp.concatenate([p_v[m, dcols_s[m, k, h]].reshape(M * SR, 128) for k in range(2)], axis=1)

    def compute(m):
        for h in range(HB):
            both = [jnp.concatenate([w[m, h, 0], w[m, h, 1]], axis=0) for w in (gate_v, up_v)]
            ab = dot(picked_in(m, h), jnp.concatenate(both, axis=1))
            a, b = ab[:, :128], ab[:, 128:]
            q = dot(picked_out(m, h), dt_v[m, h])
            sig = jax.nn.sigmoid(a)
            act = a * sig
            hid = (act * b).astype(BF)
            prod = hid.astype(F32) * q
            gsum_v[...] = prod if h == 0 else gsum_v[...] + prod
            ub = (q * act).astype(BF)
            ga = (q * b * sig * (1.0 + a * (1.0 - sig))).astype(BF)
            h_v[m, h] = hid
            a_v[m, h] = ga
            u_v[m, h] = ub
            r = dot(jnp.concatenate([ga, ub], axis=1), wt_v[m, h])
            for k in range(2):
                terms_v[2 * h + k] = r[:, k * 128 : (k + 1) * 128].reshape(2, M // 2 * SR, 128)

        def gathered(f, core):
            acc = jnp.zeros((M // 2 * SR, 128), F32)
            for h in range(HB):
                acc += terms_v[table_s[(m * HB + h) * NB + f], core]
            return acc.reshape(RING, SR, 128)

        @pl.loop(0, NB)
        def _(f):
            part[m][f] = gathered(f, oc).astype(BF)

        go(core_copy, m)

        @pl.loop(0, NB)
        def _(f):
            own[m][f] = gathered(f, c)

    def score_part(m):
        s = scol_v[m].reshape(M * SR, 128)[:, :1]
        total = jnp.sum(gsum_v[...], axis=1, keepdims=True) / jnp.where(s > 0.0, s, 1.0)
        gsx_send[m : m + 1, :cap] = jnp.sum(jnp.where(slot_mask(m), total, 0.0), axis=0, keepdims=True)

    def block_grads(m):
        @pl.loop(0, HB)
        def _(h):
            both = dot(picked_in(m, h), jnp.concatenate([a_v[m, h], u_v[m, h]], axis=1), ((0,), (0,)))
            down = dot(h_v[m, h], picked_out(m, h), ((0,), (0,)))
            for k in range(2):
                gg_out[m, h, k] = both[k * 128 : (k + 1) * 128, :128]
                gu_out[m, h, k] = both[k * 128 : (k + 1) * 128, 128:]
                gd_out[m, h, k] = down[:, k * 128 : (k + 1) * 128]

    def core_copy(m):
        return pltpu.make_async_remote_copy(
            src_ref=part[m], dst_ref=sib[m], send_sem=sib_send.at[m, 8], recv_sem=sib_recv.at[m, 8],
            device_id=sibling, device_id_type=MESH,
        )

    HA, HBH = slice(0, NB // 2), slice(NB // 2, NB)

    def rs_copy(m, k):
        return pltpu.make_async_remote_copy(
            src_ref=hop_send.at[m, k], dst_ref=hop_recv.at[m, k], send_sem=rs_send.at[m, k],
            recv_sem=rs_recv.at[m, k], device_id=left if k % 2 else right, device_id_type=MESH,
        )

    def pair_sum(m, step, half):
        xx = (x + step) % RING
        return own[m][half, xx] + sib[m][half, xx].astype(F32)

    def rs_start(m):
        got(core_copy, m)
        for k, step, half in ((0, 2, HA), (1, 2, HBH), (2, 1, HBH), (3, 3, HA)):
            hop_send[m, k] = pair_sum(m, step, half).astype(BF)
            go(rs_copy, m, k)

    def rs_middle(m):
        for k, step, half in ((4, 1, HA), (5, 3, HBH)):
            got(rs_copy, m, k - 4)
            hop_send[m, k] = (pair_sum(m, step, half) + hop_recv[m, k - 4].astype(F32)).astype(BF)
            go(rs_copy, m, k)

    def rs_finish(m):
        for k in (2, 3, 4, 5):
            got(rs_copy, m, k)
        half = NB // 2
        fst_v[:half] = (pair_sum(m, 0, HA) + hop_recv[m, 4].astype(F32) + hop_recv[m, 3].astype(F32)).astype(BF)
        fst_v[half:] = (pair_sum(m, 0, HBH) + hop_recv[m, 2].astype(F32) + hop_recv[m, 5].astype(F32)).astype(BF)
        shape = (16 * G, 8 * SR)
        row, col = iota(shape, 0), iota(shape, 1)
        pick = as_bf(col == ((row >> 1) & 7) * SR + (row >> 4) * 2 + (row & 1))
        for i in range(O // 128):
            lanes = jnp.concatenate([fst_v[o * (O // 128) + i] for o in range(8)], axis=0)
            send2[m, :, :, i * 128 : (i + 1) * 128] = dot(pick, lanes).astype(BF).reshape(G, 16, 128)
        go_all(p2_copy, G, m)
        back[m][e] = send2[m, e]

    def token_part(m):
        got(p2_copy, m)
        shape = (8 * E2, 16 * G)
        row, col = iota(shape, 0), iota(shape, 1)
        o, j, g = row >> log2(E2), (row >> log2(G)) & 1, row & (G - 1)
        vals = dot(as_bf(col == g * 16 + o * 2 + j), back[m][...].reshape(16 * G, O)).astype(BF)
        for o in range(8):
            lanes = slice(o * O, (o + 1) * O)
            rows = dot(hotm_v[m], vals[o * E2 : (o + 1) * E2], ((0,), (0,)))
            if m == 0:
                gt_v[:, lanes] = rows
            else:
                gt_out[:, lanes] = (gt_v[:, lanes] + rows).astype(BF)

    def scores_start():
        gsx_recv[d] = gsx_send[...]
        go_all(gs_copy, M)

    def scores_finish():
        got(gs_copy)
        gs = gsx_recv[0]
        for i in range(1, M):
            gs = gs + gsx_recv[i]
        gs_out[...] = gs[:2, :cap]

    def gs_copy(i):
        return pltpu.make_async_remote_copy(
            src_ref=gsx_send, dst_ref=gsx_recv.at[d], send_sem=gs_send.at[i], recv_sem=gs_recv.at[i],
            device_id=(e, (d + i) % M), device_id_type=MESH,
        )

    run = functools.partial
    stages = (
        prepare, run(retile, 0), run(ag_start, 0), run(retile, 1), run(ag_relay, 0), run(ag_start, 1), run(ag_finish, 0),
        run(compute, 0), run(ag_relay, 1), run(rs_start, 0), run(score_part, 0), run(block_grads, 0), run(rs_middle, 0),
        run(ag_finish, 1), run(compute, 1), run(score_part, 1), scores_start, run(rs_finish, 0), run(rs_start, 1),
        run(block_grads, 1), run(rs_middle, 1), run(token_part, 0), run(rs_finish, 1), scores_finish, run(token_part, 1),
    )
    for stage in stages:
        stage()

    for wait in leaving:
        wait()


def write_out(*refs):
    n = len(refs) // 2
    copies = [pltpu.make_async_copy(src, dst, refs[-1].at[k]) for k, (src, dst) in enumerate(zip(refs[:n], refs[n:]))]
    for cp in copies:
        cp.start()
    for cp in copies:
        cp.wait()


def on_device(tokens, grad_out, scores, chosen, gate_vals, up_vals, down_vals, gate_rows, down_cols):
    G, M = lax.axis_size("expert"), lax.axis_size("dp")
    T, D = tokens.shape
    HB = gate_vals.shape[1]
    cap = chosen.shape[1]
    dims = (G, M, D, T, HB)
    E2, SR, O, Q, NB = 2 * G, 2 * G, D // 8, D // 4, D // 128
    rows = M * SR
    hbm, vmem = (pl.BlockSpec(memory_space=s) for s in (pl.ANY, pltpu.VMEM))
    dma = pltpu.SemaphoreType.DMA
    sds, V = jax.ShapeDtypeStruct, pltpu.VMEM
    shapes = [((T, D), BF)] + [(gate_vals.shape, F32)] * 3 + [((2, cap), F32)]
    gate_rows, down_cols = (jnp.swapaxes(a, 1, 2) for a in (gate_rows, down_cols))
    args = (chosen, scores, gate_rows, down_cols, tokens, grad_out, gate_vals, up_vals, down_vals)
    results = pl.pallas_call(
        functools.partial(exchange, dims),
        out_shape=tuple(V(*s) for s in shapes),
        in_specs=[hbm] * 9,
        out_specs=(vmem,) * 5,
        scratch_shapes=[
            V(chosen.shape, I32),
            V((2, cap), F32),
            pltpu.SMEM(gate_rows.shape, I32),
            pltpu.SMEM(gate_rows.shape, I32),
            pltpu.SMEM((2 * HB * NB,), I32),
            V((T, D), BF),
            V((T, D), BF),
            V(gate_vals.shape, BF),
            V(gate_vals.shape, BF),
            V(gate_vals.shape, BF),
            V((2, HB, 256, 256), BF),
            V((2, HB, 256, 128), BF),
            V((2 * E2, T), BF),
            V((2, E2, T), BF),
            V((8, 4 * G, Q), BF),
            V(chosen.shape, I32),
            V((2, M, SR, 128), F32),
            V((rows, 128), F32),
            V((2 * HB + 1, 2, rows // 2, 128), F32),
            V((2, HB, rows, 128), BF),
            V((2, HB, rows, 128), BF),
            V((2, HB, rows, 128), BF),
            V((2, NB, M, SR, 128), BF),
            V((8, 128), F32),
            V((M, 8, 128), F32),
            V((T, D), F32),
        ]
        + [V((G, 16, Q), BF)] * 4
        + [V((NB, M, 2 * SR, 128), BF)] * 2
        + [V((NB, RING, SR, 128), BF)] * 2
        + [V((NB, RING, SR, 128), F32)] * 2
        + [V((NB, RING, SR, 128), BF)] * 2
        + [V((2, 6, NB // 2, SR, 128), BF)] * 2
        + [V((NB, SR, 128), BF), V((2, G, 16, O), BF)]
        + [V((G, 16, O), BF)] * 2
        + [dma((9,))]
        + [dma((2, G))] * 2
        + [dma((2, 6))] * 2
        + [dma((2, 9))] * 2
        + [dma((2, 6))] * 2
        + [dma((2, G))] * 2
        + [dma((M,))] * 2,
        compiler_params=pltpu.CompilerParams(
            collective_id=0, has_side_effects=True, vmem_limit_bytes=44 * 1024 * 1024
        ),
        name="exchange",
    )(*(pltpu.with_memory_space_constraint(a, pltpu.HBM) for a in args))
    return pl.pallas_call(
        write_out,
        out_shape=tuple(sds(*s) for s in shapes),
        in_specs=[vmem] * 5,
        out_specs=(hbm,) * 5,
        scratch_shapes=[dma((5,))],
        compiler_params=pltpu.CompilerParams(vmem_limit_bytes=16 * 1024 * 1024),
        name="write_out",
    )(*(pltpu.with_memory_space_constraint(r, pltpu.VMEM) for r in results))


def solution(mesh):
    rows = P(("expert", "dp"), None)
    blocks = P("expert", "dp", None, None, None)
    links = P("expert", "dp", None)
    return jax.shard_map(
        on_device,
        mesh=mesh,
        in_specs=(rows, rows, P("expert", None), P(), blocks, blocks, blocks, links, links),
        out_specs=(rows, blocks, blocks, blocks, P("expert", None)),
        check_vma=False,
    )
```

time: 81.7 us -> 62.3 us (0.76)
  local copies, waits for them, and re-layouts: 11.8 us -> 0 us
  Pallas kernels: 68.4 us -> 61.3 us
    unnamed x19 -> x0, local copies, waits for them, and re-layouts: 11.8 us -> none
    pallas_call x2, Pallas kernels: 68.4 us -> 61.3 us  [the longest x1 58.2 us: on_device(): pl.pallas_call(functools.partial(exchange, dims), out_shape=tuple((V(*s)...]
where the time goes in v2:
time: 62.3 us; the launch traced here: 61.9 us
  Pallas kernels  61.3 us (98%)
  between operations  0.64 us (1%)
    pallas_call x1, Pallas kernels, on_device(): pl.pallas_call(functools.partial(exchange, dims), out_shape=tuple((V(*s)...  58.2 us
    pallas_call x1, Pallas kernels, on_device(): pl.pallas_call(write_out, out_shape=tuple((sds(*s) for s in shapes)), in_...  3.09 us

profile of v2, /device:TPU:0, one launch (start us, length us, event | category | flops | bytes accessed | tf_op | source)
XLA Modules:
  0.0 61.9 jit_solution(16977107971850305704)
XLA Ops:
  0.6 58.2 %exchange.1 = (bf16[256,2048]{1,0:T(8,128)(2,1)S(1)}, f32[2,8,2,128,128]{4,3,2,1,0:T(8,128)S(1)}, f32[2,8,2,128,128]{4,3,2,1,0:T(8,128)S(1)}, f32[2,8,2,128,128]{4,3,2,1,0:T(8,128)S(1)}, f32[2,128]{1,0:T(2,128)S(1)}) custom-call(s32[32,128]{1,0:T(8,128)} %chosen_hbm.1, f32[2,128]{1,0:T(2,128)} %scores_hbm.1, s32[2,2,8]{2,1,0:T(2,128)} %bitcast.2, ...), custom_call_target="tpu_custom_call" | custom-call | tf_op jit(solution)/shard_map/exchange/pallas_call | solution.py:442
  58.8 3.1 %write_out.1 = (bf16[256,2048]{1,0:T(8,128)(2,1)}, f32[2,8,2,128,128]{4,3,2,1,0:T(8,128)}, f32[2,8,2,128,128]{4,3,2,1,0:T(8,128)}, f32[2,8,2,128,128]{4,3,2,1,0:T(8,128)}, f32[2,128]{1,0:T(2,128)}) custom-call(bf16[256,2048]{1,0:T(8,128)(2,1)S(1)} %get-tuple-element.10.refs_0_, f32[2,8,2,128,128]{4,3,2,1,0:T(8,128)S(1)} %get-tuple-element.11.refs_1_, ...), custom_call_target="tpu_custom_call" | custom-call | tf_op jit(solution)/shard_map/write_out/pallas_call | solution.py:495

commit v3 on v2

--- a/solution.py
+++ b/solution.py
@@ -170,6 +170,7 @@
             pick = as_bf(col == (row >> log2(G)) * E2 + (row & (G - 1)) * 2 + m)
             hotm_v[m] = dot(pick, hot_v[...]).astype(BF)
 
+    def prepare_table():
         @pl.loop(0, 2 * HB)
         def _(i):
             m, h = i // HB, i % HB
@@ -179,6 +180,7 @@
                 n1 = (1 - n0) * same_int(g1, f)
                 table_s[i * NB + f] = 2 * HB - n0 * (2 * HB - 2 * h) - n1 * (2 * HB - 2 * h - 1)
 
+    def prepare_weights():
         for cp in loads[6:]:
             cp.wait()
 
@@ -258,12 +260,14 @@
         got(ag, m, 3)
         go(sb, m, 5)
 
-    def ag_finish(m):
+    def ag_opposite(m):
         scale(m, (b_own, b_left, b_right))
         got(ag, m, 4)
         go(sb, m, 6)
         got(ag, m, 5)
         go(sb, m, 7)
+
+    def ag_finish(m):
         for k in range(8):
             got(sb, m, k)
         scale(m, (b_opp,) + tuple(oc * RING + i for i in range(RING)))
@@ -275,7 +279,7 @@
     def picked_out(m, h):
         return jnp.concatenate([p_v[m, dcols_s[m, k, h]].reshape(M * SR, 128) for k in range(2)], axis=1)
 
-    def compute(m):
+    def chain(m):
         for h in range(HB):
             both = [jnp.concatenate([w[m, h, 0], w[m, h, 1]], axis=0) for w in (gate_v, up_v)]
             ab = dot(picked_in(m, h), jnp.concatenate(both, axis=1))
@@ -295,29 +299,31 @@
             for k in range(2):
                 terms_v[2 * h + k] = r[:, k * 128 : (k + 1) * 128].reshape(2, M // 2 * SR, 128)
 
-        def gathered(f, core):
-            acc = jnp.zeros((M // 2 * SR, 128), F32)
-            for h in range(HB):
-                acc += terms_v[table_s[(m * HB + h) * NB + f], core]
-            return acc.reshape(RING, SR, 128)
-
-        @pl.loop(0, NB)
+    def gathered(m, f, core):
+        acc = terms_v[table_s[m * HB * NB + f], core]
+        for h in range(1, HB):
+            acc += terms_v[table_s[(m * HB + h) * NB + f], core]
+        return acc.reshape(RING, SR, 128)
+
+    def sum_away(m):
+        @pl.loop(0, NB, unroll=2)
         def _(f):
-            part[m][f] = gathered(f, oc).astype(BF)
+            part[m][f] = gathered(m, f, oc).astype(BF)
 
         go(core_copy, m)
 
-        @pl.loop(0, NB)
+    def sum_own(m):
+        @pl.loop(0, NB, unroll=2)
         def _(f):
-            own[m][f] = gathered(f, c)
+            own[m][f] = gathered(m, f, c)
 
     def score_part(m):
         s = scol_v[m].reshape(M * SR, 128)[:, :1]
         total = jnp.sum(gsum_v[...], axis=1, keepdims=True) / jnp.where(s > 0.0, s, 1.0)
         gsx_send[m : m + 1, :cap] = jnp.sum(jnp.where(slot_mask(m), total, 0.0), axis=0, keepdims=True)
 
-    def block_grads(m):
-        @pl.loop(0, HB)
+    def block_grads(m, lo, hi):
+        @pl.loop(lo, hi)
         def _(h):
             both = dot(picked_in(m, h), jnp.concatenate([a_v[m, h], u_v[m, h]], axis=1), ((0,), (0,)))
             down = dot(h_v[m, h], picked_out(m, h), ((0,), (0,)))
@@ -404,10 +410,14 @@
 
     run = functools.partial
     stages = (
-        prepare, run(retile, 0), run(ag_start, 0), run(retile, 1), run(ag_relay, 0), run(ag_start, 1), run(ag_finish, 0),
-        run(compute, 0), run(ag_relay, 1), run(rs_start, 0), run(score_part, 0), run(block_grads, 0), run(rs_middle, 0),
-        run(ag_finish, 1), run(compute, 1), run(score_part, 1), scores_start, run(rs_finish, 0), run(rs_start, 1),
-        run(block_grads, 1), run(rs_middle, 1), run(token_part, 0), run(rs_finish, 1), scores_finish, run(token_part, 1),
+        prepare, run(retile, 0), run(ag_start, 0), prepare_weights, run(retile, 1), run(ag_start, 1), prepare_table,
+        run(ag_relay, 0), run(ag_relay, 1), run(ag_opposite, 0), run(ag_finish, 0),
+        run(chain, 0), run(score_part, 0), run(ag_opposite, 1), run(sum_away, 0), run(sum_own, 0), run(ag_finish, 1),
+        run(chain, 1), run(sum_away, 1), run(sum_own, 1),
+        run(rs_start, 0), run(rs_start, 1), run(score_part, 1), scores_start, run(block_grads, 0, 0, HB // 2),
+        run(rs_middle, 0), run(rs_middle, 1), run(block_grads, 0, HB // 2, HB),
+        run(rs_finish, 0), run(rs_finish, 1), run(block_grads, 1, 0, HB), scores_finish,
+        run(token_part, 0), run(token_part, 1),
     )
     for stage in stages:
         stage()

time: 62.3 us -> 61 us (0.979)
  Pallas kernels: 61.3 us -> 60.2 us
    pallas_call x1, Pallas kernels: 58.2 us -> 57.1 us  [on_device(): pl.pallas_call(functools.partial(exchange, dims), out_shape=tuple((V(*s)...]
where the time goes in v3:
time: 61 us; the launch traced here: 60.9 us
  Pallas kernels  60.2 us (99%)
  between operations  0.64 us (1%)
    pallas_call x1, Pallas kernels, on_device(): pl.pallas_call(functools.partial(exchange, dims), out_shape=tuple((V(*s)...  57.1 us
    pallas_call x1, Pallas kernels, on_device(): pl.pallas_call(write_out, out_shape=tuple((sds(*s) for s in shapes)), in_...  3.09 us

profile of v3, /device:TPU:0, one launch (start us, length us, event | category | flops | bytes accessed | tf_op | source)
XLA Modules:
  0.0 60.9 jit_solution(17923273995721316663)
XLA Ops:
  0.6 57.1 %exchange.1 = (bf16[256,2048]{1,0:T(8,128)(2,1)S(1)}, f32[2,8,2,128,128]{4,3,2,1,0:T(8,128)S(1)}, f32[2,8,2,128,128]{4,3,2,1,0:T(8,128)S(1)}, f32[2,8,2,128,128]{4,3,2,1,0:T(8,128)S(1)}, f32[2,128]{1,0:T(2,128)S(1)}) custom-call(s32[32,128]{1,0:T(8,128)} %chosen_hbm.1, f32[2,128]{1,0:T(2,128)} %scores_hbm.1, s32[2,2,8]{2,1,0:T(2,128)} %bitcast.2, ...), custom_call_target="tpu_custom_call" | custom-call | tf_op jit(solution)/shard_map/exchange/pallas_call | solution.py:452
  57.8 3.1 %write_out.1 = (bf16[256,2048]{1,0:T(8,128)(2,1)}, f32[2,8,2,128,128]{4,3,2,1,0:T(8,128)}, f32[2,8,2,128,128]{4,3,2,1,0:T(8,128)}, f32[2,8,2,128,128]{4,3,2,1,0:T(8,128)}, f32[2,128]{1,0:T(2,128)}) custom-call(bf16[256,2048]{1,0:T(8,128)(2,1)S(1)} %get-tuple-element.10.refs_0_, f32[2,8,2,128,128]{4,3,2,1,0:T(8,128)S(1)} %get-tuple-element.11.refs_1_, ...), custom_call_target="tpu_custom_call" | custom-call | tf_op jit(solution)/shard_map/write_out/pallas_call | solution.py:505

commit v4 on v3

--- a/solution.py
+++ b/solution.py
@@ -148,10 +148,10 @@
     want = ((row >> 1) & 7) * (2 * E2) + (row & 1) * E2 + (row >> 4) * 2
     for m in range(2):
         send1[m][...] = dot(as_bf(col == want + m), stacked).astype(BF).reshape(G, 16, Q)
+        recv1[m][e] = send1[m][e]
         if m == 0:
             pl.semaphore_wait(barrier, G - 1 + M - 1)
-        go_all(p1_copy, G, m)
-        recv1[m][e] = send1[m][e]
+            go_all(p1_copy, G, 0)
     for cp in loads[6:]:
         cp.start()
 
@@ -410,13 +410,13 @@
 
     run = functools.partial
     stages = (
-        prepare, run(retile, 0), run(ag_start, 0), prepare_weights, run(retile, 1), run(ag_start, 1), prepare_table,
+        prepare, run(retile, 0), run(ag_start, 0), run(go_all, p1_copy, G, 1), prepare_table, prepare_weights, run(retile, 1), run(ag_start, 1),
         run(ag_relay, 0), run(ag_relay, 1), run(ag_opposite, 0), run(ag_finish, 0),
         run(chain, 0), run(score_part, 0), run(ag_opposite, 1), run(sum_away, 0), run(sum_own, 0), run(ag_finish, 1),
-        run(chain, 1), run(sum_away, 1), run(sum_own, 1),
-        run(rs_start, 0), run(rs_start, 1), run(score_part, 1), scores_start, run(block_grads, 0, 0, HB // 2),
-        run(rs_middle, 0), run(rs_middle, 1), run(block_grads, 0, HB // 2, HB),
-        run(rs_finish, 0), run(rs_finish, 1), run(block_grads, 1, 0, HB), scores_finish,
+        run(rs_start, 0), run(chain, 1), run(sum_away, 1), run(rs_middle, 0), run(sum_own, 1),
+        run(rs_start, 1), run(score_part, 1), scores_start, run(block_grads, 0, 0, HB // 2),
+        run(rs_middle, 1), run(rs_finish, 0), run(block_grads, 0, HB // 2, HB),
+        run(rs_finish, 1), run(block_grads, 1, 0, HB), scores_finish,
         run(token_part, 0), run(token_part, 1),
     )
     for stage in stages:

time: 61 us -> 60.3 us (0.989)
  Pallas kernels: 60.2 us -> 59.5 us
    pallas_call x1, Pallas kernels: 57.1 us -> 56.4 us  [on_device(): pl.pallas_call(functools.partial(exchange, dims), out_shape=tuple((V(*s)...]
where the time goes in v4:
time: 60.3 us; the launch traced here: 60.1 us
  Pallas kernels  59.5 us (99%)
  between operations  0.64 us (1%)
    pallas_call x1, Pallas kernels, on_device(): pl.pallas_call(functools.partial(exchange, dims), out_shape=tuple((V(*s)...  56.4 us
    pallas_call x1, Pallas kernels, on_device(): pl.pallas_call(write_out, out_shape=tuple((sds(*s) for s in shapes)), in_...  3.09 us

profile of v4, /device:TPU:0, one launch (start us, length us, event | category | flops | bytes accessed | tf_op | source)
XLA Modules:
  0.0 60.1 jit_solution(10497520006524993476)
XLA Ops:
  0.6 56.4 %exchange.1 = (bf16[256,2048]{1,0:T(8,128)(2,1)S(1)}, f32[2,8,2,128,128]{4,3,2,1,0:T(8,128)S(1)}, f32[2,8,2,128,128]{4,3,2,1,0:T(8,128)S(1)}, f32[2,8,2,128,128]{4,3,2,1,0:T(8,128)S(1)}, f32[2,128]{1,0:T(2,128)S(1)}) custom-call(s32[32,128]{1,0:T(8,128)} %chosen_hbm.1, f32[2,128]{1,0:T(2,128)} %scores_hbm.1, s32[2,2,8]{2,1,0:T(2,128)} %bitcast.2, ...), custom_call_target="tpu_custom_call" | custom-call | tf_op jit(solution)/shard_map/exchange/pallas_call | solution.py:452
  57.0 3.1 %write_out.1 = (bf16[256,2048]{1,0:T(8,128)(2,1)}, f32[2,8,2,128,128]{4,3,2,1,0:T(8,128)}, f32[2,8,2,128,128]{4,3,2,1,0:T(8,128)}, f32[2,8,2,128,128]{4,3,2,1,0:T(8,128)}, f32[2,128]{1,0:T(2,128)}) custom-call(bf16[256,2048]{1,0:T(8,128)(2,1)S(1)} %get-tuple-element.10.refs_0_, f32[2,8,2,128,128]{4,3,2,1,0:T(8,128)S(1)} %get-tuple-element.11.refs_1_, ...), custom_call_target="tpu_custom_call" | custom-call | tf_op jit(solution)/shard_map/write_out/pallas_call | solution.py:505

commit v5 on v4

--- a/solution.py
+++ b/solution.py
@@ -289,7 +289,7 @@
             act = a * sig
             hid = (act * b).astype(BF)
             prod = hid.astype(F32) * q
-            gsum_v[...] = prod if h == 0 else gsum_v[...] + prod
+            gsum_v[m] = prod if h == 0 else gsum_v[m] + prod
             ub = (q * act).astype(BF)
             ga = (q * b * sig * (1.0 + a * (1.0 - sig))).astype(BF)
             h_v[m, h] = hid
@@ -319,7 +319,7 @@
 
     def score_part(m):
         s = scol_v[m].reshape(M * SR, 128)[:, :1]
-        total = jnp.sum(gsum_v[...], axis=1, keepdims=True) / jnp.where(s > 0.0, s, 1.0)
+        total = jnp.sum(gsum_v[m], axis=1, keepdims=True) / jnp.where(s > 0.0, s, 1.0)
         gsx_send[m : m + 1, :cap] = jnp.sum(jnp.where(slot_mask(m), total, 0.0), axis=0, keepdims=True)
 
     def block_grads(m, lo, hi):
@@ -412,9 +412,9 @@
     stages = (
         prepare, run(retile, 0), run(ag_start, 0), run(go_all, p1_copy, G, 1), prepare_table, prepare_weights, run(retile, 1), run(ag_start, 1),
         run(ag_relay, 0), run(ag_relay, 1), run(ag_opposite, 0), run(ag_finish, 0),
-        run(chain, 0), run(score_part, 0), run(ag_opposite, 1), run(sum_away, 0), run(sum_own, 0), run(ag_finish, 1),
+        run(chain, 0), run(ag_opposite, 1), run(sum_away, 0), run(sum_own, 0), run(ag_finish, 1),
         run(rs_start, 0), run(chain, 1), run(sum_away, 1), run(rs_middle, 0), run(sum_own, 1),
-        run(rs_start, 1), run(score_part, 1), scores_start, run(block_grads, 0, 0, HB // 2),
+        run(rs_start, 1), run(score_part, 0), run(score_part, 1), scores_start, run(block_grads, 0, 0, HB // 2),
         run(rs_middle, 1), run(rs_finish, 0), run(block_grads, 0, HB // 2, HB),
         run(rs_finish, 1), run(block_grads, 1, 0, HB), scores_finish,
         run(token_part, 0), run(token_part, 1),
@@ -472,7 +472,7 @@
             V((8, 4 * G, Q), BF),
             V(chosen.shape, I32),
             V((2, M, SR, 128), F32),
-            V((rows, 128), F32),
+            V((2, rows, 128), F32),
             V((2 * HB + 1, 2, rows // 2, 128), F32),
             V((2, HB, rows, 128), BF),
             V((2, HB, rows, 128), BF),

time: 60.3 us -> 60.3 us (level)
  no operation moved by 1% of the time
where the time goes in v5:
time: 60.3 us; the launch traced here: 60.1 us
  Pallas kernels  59.5 us (99%)
  between operations  0.64 us (1%)
    pallas_call x1, Pallas kernels, on_device(): pl.pallas_call(functools.partial(exchange, dims), out_shape=tuple((V(*s)...  56.4 us
    pallas_call x1, Pallas kernels, on_device(): pl.pallas_call(write_out, out_shape=tuple((sds(*s) for s in shapes)), in_...  3.09 us

profile of v5, /device:TPU:0, one launch (start us, length us, event | category | flops | bytes accessed | tf_op | source)
XLA Modules:
  0.0 60.1 jit_solution(16800768483239448108)
XLA Ops:
  0.6 56.4 %exchange.1 = (bf16[256,2048]{1,0:T(8,128)(2,1)S(1)}, f32[2,8,2,128,128]{4,3,2,1,0:T(8,128)S(1)}, f32[2,8,2,128,128]{4,3,2,1,0:T(8,128)S(1)}, f32[2,8,2,128,128]{4,3,2,1,0:T(8,128)S(1)}, f32[2,128]{1,0:T(2,128)S(1)}) custom-call(s32[32,128]{1,0:T(8,128)} %chosen_hbm.1, f32[2,128]{1,0:T(2,128)} %scores_hbm.1, s32[2,2,8]{2,1,0:T(2,128)} %bitcast.2, ...), custom_call_target="tpu_custom_call" | custom-call | tf_op jit(solution)/shard_map/exchange/pallas_call | solution.py:452
  57.0 3.1 %write_out.1 = (bf16[256,2048]{1,0:T(8,128)(2,1)}, f32[2,8,2,128,128]{4,3,2,1,0:T(8,128)}, f32[2,8,2,128,128]{4,3,2,1,0:T(8,128)}, f32[2,8,2,128,128]{4,3,2,1,0:T(8,128)}, f32[2,128]{1,0:T(2,128)}) custom-call(bf16[256,2048]{1,0:T(8,128)(2,1)S(1)} %get-tuple-element.10.refs_0_, f32[2,8,2,128,128]{4,3,2,1,0:T(8,128)S(1)} %get-tuple-element.11.refs_1_, ...), custom_call_target="tpu_custom_call" | custom-call | tf_op jit(solution)/shard_map/write_out/pallas_call | solution.py:505
